TPU v7x, 32 devices: a whole 2x2x4 slice. The times are simulated.
32 devices in a mesh: ulysses: 4 (over y, x), blk: 8 (over z, core).
Axes of the slice: x: 2, y: 2, z: 4, core: 2. Of those that a mesh axis runs over, the one named last changes fastest.
Arguments:
- tokens: bfloat16 [4096, 1024], P(('ulysses', 'blk')), may hold values from -6 to 6
- ln1_gain: bfloat16 [1024], P(('ulysses', 'blk')), may hold values from 0.5 to 1.5
- ln1_bias: bfloat16 [1024], P(('ulysses', 'blk')), may hold values from -1.75 to 1.75
- qkv_weight: bfloat16 [1024, 3072], P(('ulysses', 'blk')), may hold values from -0.1875 to 0.1875
- qv_bias: bfloat16 [2048], P(('ulysses', 'blk')), may hold values from -0.625 to 0.625
- proj_weight: bfloat16 [1024, 1024], P(('ulysses', 'blk')), may hold values from -1.5 to 1.5
- proj_bias: bfloat16 [1024], P(('ulysses', 'blk')), may hold values from -1.75 to 1.75
- ln2_gain: bfloat16 [1024], P(('ulysses', 'blk')), may hold values from 0.5 to 1.5
- ln2_bias: bfloat16 [1024], P(('ulysses', 'blk')), may hold values from -1.75 to 1.75
- up_weight: bfloat16 [1024, 4096], P(('ulysses', 'blk')), may hold values from -0.1875 to 0.1875
- up_bias: bfloat16 [4096], P(('ulysses', 'blk')), may hold values from -1.75 to 1.75
- down_weight: bfloat16 [4096, 1024], P(('ulysses', 'blk')), may hold values from -0.09375 to 0.09375
- down_bias: bfloat16 [1024], P(('ulysses', 'blk')), may hold values from -1.75 to 1.75
- alibi_slopes: float32 [16], replicated, may hold values from 0 to 1
- doc_starts: int32 [7], replicated, may hold values from 0 to 3584, as said below
- cotangent: bfloat16 [4096, 1024], P(('ulysses', 'blk')), may hold values from -12 to 12
Outputs:
- output: bfloat16 [4096, 1024], P(('ulysses', 'blk'))
- input_grad: bfloat16 [4096, 1024], P(('ulysses', 'blk'))
- ln1_gain_grad: float32 [1024], P(('ulysses', 'blk'))
- ln1_bias_grad: float32 [1024], P(('ulysses', 'blk'))
- qkv_weight_grad: float32 [1024, 3072], P(('ulysses', 'blk'))
- qv_bias_grad: float32 [2048], P(('ulysses', 'blk'))
- proj_weight_grad: float32 [1024, 1024], P(('ulysses', 'blk'))
- proj_bias_grad: float32 [1024], P(('ulysses', 'blk'))
- ln2_gain_grad: float32 [1024], P(('ulysses', 'blk'))
- ln2_bias_grad: float32 [1024], P(('ulysses', 'blk'))
- up_weight_grad: float32 [1024, 4096], P(('ulysses', 'blk'))
- up_bias_grad: float32 [4096], P(('ulysses', 'blk'))
- down_weight_grad: float32 [4096, 1024], P(('ulysses', 'blk'))
- down_bias_grad: float32 [1024], P(('ulysses', 'blk'))
Inputs may be any that keep to these rules, and one draw needn't show every extreme that they name: `doc_starts`: strictly increasing, the first entry 0, the last entry exactly 3584. Document d holds the tokens from entry d up to the next entry, the last one up to the end. No document is longer than 1024 tokens, and one is exactly 1024 tokens long.
All inputs are finite; a program needn't handle non-finite values.
Results may differ from a plain program's by a relative error of at most 0.017.
Values may be sent and summed in bfloat16 or wider, within the bound.
A program may use at most 256 MiB of HBM per device.

v0:
```python
import jax
import jax.numpy as jnp
from jax import lax
from jax.sharding import PartitionSpec as P

HEADS = 16
HEAD_DIM = 64


def layer_norm(values, norm_gain, norm_shift):
    center = jnp.mean(values, axis=-1, keepdims=True)
    offset = values - center
    spread = jnp.mean(offset * offset, axis=-1, keepdims=True)
    return offset * lax.rsqrt(spread + 1e-05) * norm_gain + norm_shift


def gelu_tanh(values):
    return (
        0.5
        * values
        * (1.0 + jnp.tanh(0.7978845608028654 * (values + 0.044715 * values * values * values)))
    )


def place_rows(local_rows, team_size, blk_count, tok_rows):
    team_span = team_size * tok_rows
    return (
        local_rows % team_span // tok_rows * blk_count + local_rows // team_span
    ) * tok_rows + local_rows % tok_rows


def doc_index(positions, doc_starts):
    return jnp.sum((positions[:, None] >= doc_starts[None, :]).astype(jnp.int32), axis=1) - 1


def split_rows(row_count, step_rows):
    return (row_count // step_rows, step_rows)


def score_block(queries, keys, query_pos, key_pos, query_doc, key_doc, slopes):
    raw_scores = jnp.einsum(
        "qhd,khd->hqk", queries, keys, preferred_element_type=jnp.float32
    ) * HEAD_DIM ** (-0.5)
    distance = (query_pos[:, None] - key_pos[None, :]).astype(jnp.float32)
    raw_scores = raw_scores - slopes[:, None, None] * distance[None]
    allowed = (key_pos[None, :] <= query_pos[:, None]) & (query_doc[:, None] == key_doc[None, :])
    return (jnp.where(allowed[None], raw_scores, -1e30), allowed[None])


def body(
    tokens,
    ln1_gain,
    ln1_bias,
    qkv_weight,
    qv_bias,
    proj_weight,
    proj_bias,
    ln2_gain,
    ln2_bias,
    up_weight,
    up_bias,
    down_weight,
    down_bias,
    alibi_slopes,
    doc_starts,
    cotangent,
):
    team_size = lax.axis_size("ulysses")
    blk_count = lax.axis_size("blk")
    tok_rows = tokens.shape[0]
    width_all = tokens.shape[1]
    head_rows = team_size * tok_rows
    heads_here = HEADS // team_size
    features = heads_here * HEAD_DIM
    scale_factor = HEAD_DIM ** (-0.5)
    gathered = (
        lax.all_gather(ln1_gain, ("ulysses", "blk"), axis=0, tiled=True),
        lax.all_gather(ln1_bias, ("ulysses", "blk"), axis=0, tiled=True),
        lax.all_gather(qkv_weight, ("ulysses", "blk"), axis=0, tiled=True),
        lax.all_gather(qv_bias, ("ulysses", "blk"), axis=0, tiled=True),
        lax.all_gather(proj_weight, ("ulysses", "blk"), axis=0, tiled=True),
        lax.all_gather(proj_bias, ("ulysses", "blk"), axis=0, tiled=True),
        lax.all_gather(ln2_gain, ("ulysses", "blk"), axis=0, tiled=True),
        lax.all_gather(ln2_bias, ("ulysses", "blk"), axis=0, tiled=True),
        lax.all_gather(up_weight, ("ulysses", "blk"), axis=0, tiled=True),
        lax.all_gather(up_bias, ("ulysses", "blk"), axis=0, tiled=True),
        lax.all_gather(down_weight, ("ulysses", "blk"), axis=0, tiled=True),
        lax.all_gather(down_bias, ("ulysses", "blk"), axis=0, tiled=True),
    )
    gain_one = gathered[0].astype(jnp.float32)
    shift_one = gathered[1].astype(jnp.float32)
    qkv_proj = gathered[2]
    qv_shift = gathered[3].astype(jnp.float32)
    proj_mat = gathered[4]
    proj_shift = gathered[5].astype(jnp.float32)
    gain_two = gathered[6].astype(jnp.float32)
    shift_two = gathered[7].astype(jnp.float32)
    up_mat = gathered[8]
    up_shift = gathered[9].astype(jnp.float32)
    down_mat = gathered[10]
    down_shift = gathered[11].astype(jnp.float32)
    inputs_f = tokens.astype(jnp.float32)
    normed_one = layer_norm(inputs_f, gain_one, shift_one).astype(jnp.bfloat16)
    joined_bias = jnp.concatenate(
        [qv_shift[:width_all], jnp.zeros((width_all,), jnp.float32), qv_shift[width_all:]]
    )
    joined = (
        jnp.dot(normed_one, qkv_proj, preferred_element_type=jnp.float32) + joined_bias
    ).astype(jnp.bfloat16)
    head_local = lax.all_to_all(
        joined.reshape(tok_rows, 3, team_size, features),
        "ulysses",
        split_axis=2,
        concat_axis=0,
        tiled=True,
    )
    queries_flat = head_local[:, 0, 0]
    queries = queries_flat.reshape(head_rows, heads_here, HEAD_DIM)
    key_value = head_local[:, 1:, 0]
    own_keys = key_value[:, 0].reshape(head_rows, heads_here, HEAD_DIM)
    own_values = key_value[:, 1].reshape(head_rows, heads_here, HEAD_DIM)
    slopes = lax.dynamic_slice_in_dim(
        alibi_slopes, lax.axis_index("ulysses") * heads_here, heads_here, 0
    )
    own_rows = lax.axis_index("blk") * head_rows + jnp.arange(head_rows, dtype=jnp.int32)
    own_pos = place_rows(own_rows, team_size, blk_count, tok_rows)
    own_doc = doc_index(own_pos, doc_starts)
    start_state = (
        jnp.full((heads_here, head_rows), -1e30, jnp.float32),
        jnp.zeros((heads_here, head_rows), jnp.float32),
        jnp.zeros((heads_here, head_rows, HEAD_DIM), jnp.float32),
    )
    carried = start_state
    piece_rows = lax.all_gather(key_value, "blk", axis=0, tiled=True)
    number, step_rows = split_rows(piece_rows.shape[0], head_rows)
    stacked = piece_rows.reshape(number, step_rows, 2, heads_here, HEAD_DIM)
    offsets = step_rows * jnp.arange(number, dtype=jnp.int32)

    def online_step(running, inputs_pair):
        best_now, norm_sum, accumulated = running
        kv_block, offset_now = inputs_pair
        key_pos = place_rows(
            offset_now + jnp.arange(step_rows, dtype=jnp.int32), team_size, blk_count, tok_rows
        )
        key_doc = doc_index(key_pos, doc_starts)
        masked, allowed = score_block(
            queries, kv_block[:, 0], own_pos, key_pos, own_doc, key_doc, slopes
        )
        best_next = jnp.maximum(best_now, jnp.max(masked, axis=-1))
        weights = jnp.where(allowed, jnp.exp(masked - best_next[..., None]), 0.0)
        shrink = jnp.exp(best_now - best_next)
        norm_sum = norm_sum * shrink + jnp.sum(weights, axis=-1)
        accumulated = accumulated * shrink[..., None] + jnp.einsum(
            "hqk,khd->hqd",
            weights.astype(jnp.bfloat16),
            kv_block[:, 1],
            preferred_element_type=jnp.float32,
        )
        return ((best_next, norm_sum, accumulated), None)

    carried, _ = lax.scan(online_step, carried, (stacked, offsets))
    best_all, norm_all, acc_all = carried
    attended_heads = acc_all / norm_all[..., None]
    log_norm = best_all + jnp.log(norm_all)
    attended_rows = (
        attended_heads.transpose(1, 0, 2).reshape(head_rows, 1, features).astype(jnp.bfloat16)
    )
    attended = lax.all_to_all(
        attended_rows, "ulysses", split_axis=0, concat_axis=1, tiled=True
    ).reshape(tok_rows, width_all)
    mixed = inputs_f + jnp.dot(attended, proj_mat, preferred_element_type=jnp.float32) + proj_shift
    normed_two = layer_norm(mixed, gain_two, shift_two).astype(jnp.bfloat16)
    up_values = jnp.dot(normed_two, up_mat, preferred_element_type=jnp.float32) + up_shift
    activated = gelu_tanh(up_values).astype(jnp.bfloat16)
    output = (
        mixed + jnp.dot(activated, down_mat, preferred_element_type=jnp.float32) + down_shift
    ).astype(jnp.bfloat16)
    contract_rows = (((0,), (0,)), ((), ()))
    contract_cols = (((1,), (1,)), ((), ()))
    grad_out = cotangent.astype(jnp.float32)
    down_grad = lax.dot_general(
        activated, cotangent, contract_rows, preferred_element_type=jnp.float32
    )
    down_bias_grad = jnp.sum(grad_out, axis=0)
    grad_act = lax.dot_general(
        cotangent, down_mat, contract_cols, preferred_element_type=jnp.float32
    )
    _, gelu_pull = jax.vjp(gelu_tanh, up_values)
    grad_up = gelu_pull(grad_act)[0].astype(jnp.bfloat16)
    up_grad = lax.dot_general(
        normed_two, grad_up, contract_rows, preferred_element_type=jnp.float32
    )
    up_bias_grad = jnp.sum(grad_up.astype(jnp.float32), axis=0)
    grad_norm_two = lax.dot_general(
        grad_up, up_mat, contract_cols, preferred_element_type=jnp.float32
    )
    _, norm_two_pull = jax.vjp(layer_norm, mixed, gain_two, shift_two)
    grad_mixed_part, ln2_gain_grad, ln2_bias_grad = norm_two_pull(grad_norm_two)
    grad_mixed = grad_out + grad_mixed_part
    grad_branch = grad_mixed.astype(jnp.bfloat16)
    proj_grad = lax.dot_general(
        attended, grad_branch, contract_rows, preferred_element_type=jnp.float32
    )
    proj_bias_grad = jnp.sum(grad_mixed, axis=0)
    grad_att = lax.dot_general(
        grad_branch, proj_mat, contract_cols, preferred_element_type=jnp.float32
    ).astype(jnp.bfloat16)
    grad_heads = lax.all_to_all(
        grad_att.reshape(tok_rows, team_size, features),
        "ulysses",
        split_axis=1,
        concat_axis=0,
        tiled=True,
    )
    grad_heads_flat = grad_heads[:, 0]
    grad_att_heads = grad_heads_flat.reshape(head_rows, heads_here, HEAD_DIM)
    delta = jnp.sum(grad_att_heads.astype(jnp.float32).transpose(1, 0, 2) * attended_heads, axis=-1)
    carried = jnp.zeros((heads_here, head_rows, HEAD_DIM), jnp.float32)
    piece_rows = lax.all_gather(key_value, "blk", axis=0, tiled=True)
    number, query_step_rows = split_rows(piece_rows.shape[0], head_rows)
    stacked = piece_rows.reshape(number, query_step_rows, 2, heads_here, HEAD_DIM)
    offsets = query_step_rows * jnp.arange(number, dtype=jnp.int32)

    def query_step(running, inputs_pair):
        kv_block, offset_now = inputs_pair
        key_pos = place_rows(
            offset_now + jnp.arange(query_step_rows, dtype=jnp.int32),
            team_size,
            blk_count,
            tok_rows,
        )
        key_doc = doc_index(key_pos, doc_starts)
        masked, allowed = score_block(
            queries, kv_block[:, 0], own_pos, key_pos, own_doc, key_doc, slopes
        )
        probs = jnp.where(allowed, jnp.exp(masked - log_norm[..., None]), 0.0)
        grad_probs = jnp.einsum(
            "qhd,khd->hqk", grad_att_heads, kv_block[:, 1], preferred_element_type=jnp.float32
        )
        grad_scores = (probs * (grad_probs - delta[..., None])).astype(jnp.bfloat16)
        running = running + jnp.einsum(
            "hqk,khd->hqd", grad_scores, kv_block[:, 0], preferred_element_type=jnp.float32
        )
        return (running, None)

    carried, _ = lax.scan(query_step, carried, (stacked, offsets))
    grad_queries = carried * scale_factor
    all_norms, all_deltas = (
        lax.all_gather(log_norm.T, "blk", axis=0, tiled=True),
        lax.all_gather(delta.T, "blk", axis=0, tiled=True),
    )
    empty_keys = jnp.zeros((head_rows, heads_here, HEAD_DIM), jnp.float32)
    carried = (empty_keys, empty_keys)
    pieces = (
        lax.all_gather(queries_flat, "blk", axis=0, tiled=True),
        lax.all_gather(grad_heads_flat, "blk", axis=0, tiled=True),
    )
    number, key_step_rows = split_rows(pieces[0].shape[0], head_rows)
    query_stack = pieces[0].reshape(number, key_step_rows, heads_here, HEAD_DIM)
    grad_stack = pieces[1].reshape(number, key_step_rows, heads_here, HEAD_DIM)
    offsets = key_step_rows * jnp.arange(number, dtype=jnp.int32)

    def key_step(running, inputs_triple):
        grad_keys_now, grad_values_now = running
        query_block, grad_block, offset_now = inputs_triple
        query_pos = place_rows(
            offset_now + jnp.arange(key_step_rows, dtype=jnp.int32), team_size, blk_count, tok_rows
        )
        query_doc = doc_index(query_pos, doc_starts)
        norm_block = lax.dynamic_slice_in_dim(all_norms, offset_now, key_step_rows, 0).T
        delta_block = lax.dynamic_slice_in_dim(all_deltas, offset_now, key_step_rows, 0).T
        masked, allowed = score_block(
            query_block, own_keys, query_pos, own_pos, query_doc, own_doc, slopes
        )
        probs = jnp.where(allowed, jnp.exp(masked - norm_block[..., None]), 0.0)
        grad_values_now = grad_values_now + jnp.einsum(
            "hqk,qhd->khd",
            probs.astype(jnp.bfloat16),
            grad_block,
            preferred_element_type=jnp.float32,
        )
        grad_probs = jnp.einsum(
            "qhd,khd->hqk", grad_block, own_values, preferred_element_type=jnp.float32
        )
        grad_scores = (probs * (grad_probs - delta_block[..., None])).astype(jnp.bfloat16)
        grad_keys_now = grad_keys_now + jnp.einsum(
            "hqk,qhd->khd", grad_scores, query_block, preferred_element_type=jnp.float32
        )
        return ((grad_keys_now, grad_values_now), None)

    carried, _ = lax.scan(key_step, carried, (query_stack, grad_stack, offsets))
    grad_keys, grad_values = carried
    grad_pack = jnp.stack(
        [
            grad_queries.transpose(1, 0, 2).reshape(head_rows, features),
            (grad_keys * scale_factor).reshape(head_rows, features),
            grad_values.reshape(head_rows, features),
        ],
        axis=1,
    ).astype(jnp.bfloat16)
    grad_joined = lax.all_to_all(
        grad_pack.reshape(head_rows, 3, 1, features),
        "ulysses",
        split_axis=0,
        concat_axis=2,
        tiled=True,
    ).reshape(tok_rows, 3 * width_all)
    qkv_grad = lax.dot_general(
        normed_one, grad_joined, contract_rows, preferred_element_type=jnp.float32
    )
    joined_sums = jnp.sum(grad_joined.astype(jnp.float32), axis=0)
    qv_bias_grad = jnp.concatenate([joined_sums[:width_all], joined_sums[2 * width_all :]])
    grad_norm_one = lax.dot_general(
        grad_joined, qkv_proj, contract_cols, preferred_element_type=jnp.float32
    )
    _, norm_one_pull = jax.vjp(layer_norm, inputs_f, gain_one, shift_one)
    grad_inputs_part, ln1_gain_grad, ln1_bias_grad = norm_one_pull(grad_norm_one)
    input_grad = (grad_mixed + grad_inputs_part).astype(jnp.bfloat16)
    shares = (
        lax.psum_scatter(ln1_gain_grad, ("ulysses", "blk"), scatter_dimension=0, tiled=True),
        lax.psum_scatter(ln1_bias_grad, ("ulysses", "blk"), scatter_dimension=0, tiled=True),
        lax.psum_scatter(qkv_grad, ("ulysses", "blk"), scatter_dimension=0, tiled=True),
        lax.psum_scatter(qv_bias_grad, ("ulysses", "blk"), scatter_dimension=0, tiled=True),
        lax.psum_scatter(proj_grad, ("ulysses", "blk"), scatter_dimension=0, tiled=True),
        lax.psum_scatter(proj_bias_grad, ("ulysses", "blk"), scatter_dimension=0, tiled=True),
        lax.psum_scatter(ln2_gain_grad, ("ulysses", "blk"), scatter_dimension=0, tiled=True),
        lax.psum_scatter(ln2_bias_grad, ("ulysses", "blk"), scatter_dimension=0, tiled=True),
        lax.psum_scatter(up_grad, ("ulysses", "blk"), scatter_dimension=0, tiled=True),
        lax.psum_scatter(up_bias_grad, ("ulysses", "blk"), scatter_dimension=0, tiled=True),
        lax.psum_scatter(down_grad, ("ulysses", "blk"), scatter_dimension=0, tiled=True),
        lax.psum_scatter(down_bias_grad, ("ulysses", "blk"), scatter_dimension=0, tiled=True),
    )
    return (
        output,
        input_grad,
        shares[0],
        shares[1],
        shares[2],
        shares[3],
        shares[4],
        shares[5],
        shares[6],
        shares[7],
        shares[8],
        shares[9],
        shares[10],
        shares[11],
    )


def solution(mesh):
    in_specs = (
        P(("ulysses", "blk"), None),
        P(("ulysses", "blk")),
        P(("ulysses", "blk")),
        P(("ulysses", "blk"), None),
        P(("ulysses", "blk")),
        P(("ulysses", "blk"), None),
        P(("ulysses", "blk")),
        P(("ulysses", "blk")),
        P(("ulysses", "blk")),
        P(("ulysses", "blk"), None),
        P(("ulysses", "blk")),
        P(("ulysses", "blk"), None),
        P(("ulysses", "blk")),
        P(),
        P(),
        P(("ulysses", "blk"), None),
    )
    out_specs = (
        P(("ulysses", "blk"), None),
        P(("ulysses", "blk"), None),
        P(("ulysses", "blk")),
        P(("ulysses", "blk")),
        P(("ulysses", "blk"), None),
        P(("ulysses", "blk")),
        P(("ulysses", "blk"), None),
        P(("ulysses", "blk")),
        P(("ulysses", "blk")),
        P(("ulysses", "blk")),
        P(("ulysses", "blk"), None),
        P(("ulysses", "blk")),
        P(("ulysses", "blk"), None),
        P(("ulysses", "blk")),
    )
    return jax.shard_map(body, mesh=mesh, in_specs=in_specs, out_specs=out_specs, check_vma=False)
```

profile of v0, /device:TPU:0, one launch (start us, length us, event | category | flops | bytes accessed | tf_op | source)
XLA Modules:
  0.0 1262.9 jit_solution(15966023088545532491)
XLA Ops:
  13.8 42.5 %all-reduce.16 = (bf16[2048]{0:T(1024)(128)(2,1)S(1)}, bf16[1024]{0:T(1024)(128)(2,1)S(1)}, bf16[1024]{0:T(1024)(128)(2,1)S(1)}, bf16[1024]{0:T(1024)(128)(2,1)S...) all-reduce(bf16[2048]{0:T(1024)(128)(2,1)S(1)} %dynamic-update-slic, ...), channel_id=1, replica_groups=mesh['ulysses'=4,'blk'=8] {'ulysses','blk'}, use_global_device_ids=true, to_apply=%add.2 | all-reduce | flops 8192 | bytes 32768
  58.6 24.8 %all-gather.11.cloned.1.call-done = bf16[1024,3072]{1,0:T(8,128)(2,1)} async-done(((bf16[32,3072]{1,0:T(8,128)(2,1)}), bf16[1024,3072]{1,0:T(8,128)(2,1)}) %all-gather.11.cloned.1.call-update) | async-done | bytes 6291472 | tf_op jit(solution)/shard_map/all_gather | solution.py:79
  83.4 4.0 fusion.112
  88.1 14.5 %all_to_all.63 = bf16[128,3,4,256]{3,0,1,2:T(8,128)(2,1)S(1)} all-to-all(bf16[128,3,4,256]{3,0,1,2:T(8,128)(2,1)S(1)} %copy.156), channel_id=1, replica_groups=mesh['ulysses'=4,'blk'=8] {'ulysses'}, dimensions={2} | all-to-all | bytes 1572864 | tf_op jit(solution)/shard_map/all_to_all | solution.py:110
  106.0 42.9 %all-gather.21.cloned.1.call-done = bf16[4096,2,1,256]{3,0,1,2:T(8,128)(2,1)} async-done(((bf16[512,2,1,256]{3,0,1,2:T(8,128)(2,1)}), bf16[4096,2,1,256]{3,0,1,2:T(8,128)(2,1)}) %all-gather.21.cloned.1.call-update) | async-done | bytes 4194320 | tf_op jit(solution)/shard_map/all_gather | solution.py:134
  148.9 12.9 %reshape.805 = bf16[8,512,2,4,64]{4,3,1,0,2:T(4,128)(2,1)} reshape(bf16[4096,2,1,256]{3,0,1,2:T(8,128)(2,1)} %all-gather.21.cloned.1.call-done) | data formatting | bytes 8388608 | tf_op jit(solution)/shard_map/reshape | solution.py:136
  161.8 12.7 %copy.160 = bf16[8,512,2,4,64]{1,4,3,2,0:T(8,128)(2,1)} copy(bf16[8,512,2,4,64]{4,3,1,0,2:T(4,128)(2,1)} %reshape.805) | data formatting | bytes 8388608
  174.5 105.9 %while.48 = (s32[]{:T(128)}, f32[4,512]{1,0:T(4,128)S(1)}, f32[4,512]{1,0:T(4,128)S(1)}, f32[4,512,64]{1,2,0:T(8,128)}, s32[8]{0:T(128)S(1)}, /*index=5*/s32[512...) while((s32[]{:T(128)}, f32[4,512]{1,0:T(4,128)S(1)}, ...), condition=%wide.region_7.8_spmd.clone, body=%wide.region_3.7_spmd.clone.sunk | while | flops 290131456 | bytes 37643504 | solution.py:161
  180.6 3.7 fusion.209
  192.9 3.7 fusion.209
  206.3 3.7 fusion.209
  219.7 3.7 fusion.209
  233.0 3.7 fusion.209
  246.4 3.7 fusion.209
  259.7 3.7 fusion.209
  273.1 3.9 fusion.209
  287.7 40.9 %all-gather.2 = bf16[32,1,128]{2,1,0:T(2,128)(2,1)S(1)} all-gather(bf16[1,1,128]{2,1,0:T(2,128)(2,1)S(1)} %bitcast.244), channel_id=1, replica_groups=mesh['ulysses'=4,'blk'=8] {'ulysses','blk'}, dimensions={0}, use_global_device_ids=true | all-gather | bytes 8448 | tf_op jit(solution)/shard_map/all_gather | solution.py:86
  331.8 4.8 convolution_add_fusion
  336.5 28.8 %all-gather.17.cloned.1.call-done = bf16[4096,1024]{1,0:T(8,128)(2,1)} async-done(((bf16[128,1024]{1,0:T(8,128)(2,1)}), bf16[4096,1024]{1,0:T(8,128)(2,1)}) %all-gather.17.cloned.1.call-update) | async-done | bytes 8388624 | tf_op jit(solution)/shard_map/all_gather | solution.py:87
  365.3 8.3 convert_reduce_fusion.3
  377.9 9.5 all_to_all.64
  388.5 6.6 all-gather.23.cloned.1.call-done
  395.1 7.1 reshape.803
  402.1 7.1 copy.170
  409.3 14.5 %all_gather.66 = f32[4096,4]{0,1:T(4,128)S(1)} all-gather(f32[512,4]{0,1:T(4,128)S(1)} %bitcast.241), channel_id=1, replica_groups=mesh['ulysses'=4,'blk'=8] {'blk'}, dimensions={0}, use_global_device_ids=true | all-gather | bytes 73728 | tf_op jit(solution)/shard_map/all_gather | solution.py:249
  429.0 14.9 %all_gather.68 = f32[4096,4]{0,1:T(4,128)} all-gather(f32[512,4]{0,1:T(4,128)S(1)} %bitcast.240), channel_id=1, replica_groups=mesh['ulysses'=4,'blk'=8] {'blk'}, dimensions={0}, use_global_device_ids=true | all-gather | bytes 73728 | tf_op jit(solution)/shard_map/all_gather | solution.py:250
  443.9 89.8 %while.49 = (s32[]{:T(128)}, f32[4,512,64]{1,2,0:T(8,128)}, s32[8]{0:T(128)S(1)}, s32[512]{0:T(512)S(1)}, s32[7]{0:T(128)S(1)}, /*index=5*/bf16[8,512,2,4,64]{1,...) while((s32[]{:T(128)}, f32[4,512,64]{1,2,0:T(8,128)}, ...), condition=%wide.region_15.16_spmd.clone, body=%wide.region_13.15_spmd.clone.sunk | while | flops 413722112 | bytes 14459355 | solution.py:246
  449.6 5.5 fusion.216
  460.7 5.6 fusion.216
  471.9 5.6 fusion.216
  483.1 5.6 fusion.216
  494.4 5.6 fusion.216
  505.6 5.6 fusion.216
  516.9 5.6 fusion.216
  528.1 5.6 fusion.216
  534.8 7.1 reshape.804
  541.9 7.0 copy.171
  548.9 149.5 %while.50 = (s32[]{:T(128)}, f32[512,4,64]{0,2,1:T(8,128)}, f32[512,4,64]{0,2,1:T(8,128)}, bf16[8,512,4,64]{1,3,2,0:T(8,128)(2,1)}, s32[8]{0:T(128)S(1)}, /*inde...) while((s32[]{:T(128)}, f32[512,4,64]{0,2,1:T(8,128)}, ...), condition=%wide.region_18.19_spmd.clone, body=%wide.region_16.18_spmd.clone.sunk | while | flops 555542016 | bytes 24463516 | solution.py:291
  548.9 3.7 fusion.224
  557.1 5.7 fusion.226
  562.8 4.0 fusion.227
  575.7 5.8 fusion.226
  581.5 3.9 fusion.227
  594.4 5.8 fusion.226
  600.2 3.9 fusion.227
  613.1 5.8 fusion.226
  618.9 3.9 fusion.227
  631.8 5.8 fusion.226
  637.6 3.9 fusion.227
  650.5 5.8 fusion.226
  656.3 3.9 fusion.227
  669.2 5.8 fusion.226
  675.0 3.9 fusion.227
  687.9 5.8 fusion.226
  693.7 3.9 fusion.227
  701.4 18.0 %all_to_all.65 = bf16[512,3,1,256]{3,1,2,0:T(4,128)(2,1)S(1)} all-to-all(bf16[512,3,1,256]{3,1,2,0:T(4,128)(2,1)S(1)} %copy.172), channel_id=1, replica_groups=mesh['ulysses'=4,'blk'=8] {'ulysses'}, dimensions={0} | all-to-all | bytes 1572864 | tf_op jit(solution)/shard_map/all_to_all | solution.py:301
  719.9 6.4 fusion.148
  727.5 9.0 fusion.152
  738.2 9.0 fusion.154
  747.9 7.0 fusion.121
  759.0 40.1 %all-reduce.15 = (f32[1024]{0:T(1024)S(1)}, f32[1024]{0:T(1024)S(1)}, f32[2048]{0:T(1024)S(1)}, f32[1024]{0:T(1024)S(1)}, f32[1024]{0:T(1024)S(1)}, /*index=5*/f...) all-reduce(f32[1024]{0:T(1024)S(1)} %get-tuple-element.1032, ...), channel_id=4, replica_groups=mesh['ulysses'=4,'blk'=8] {'ulysses','blk'}, use_global_device_ids=true, to_apply=%region_22.23.clone | all-reduce | flops 12288 | bytes 98304
  803.8 76.4 %reduce-scatter.5.cloned.1.call-done = f32[32,3072]{1,0:T(8,128)} async-done(((f32[1024,3072]{1,0:T(8,128)}), f32[32,3072]{1,0:T(8,128)}) %reduce-scatter.5.cloned.1.call-update) | async-done | bytes 393232 | tf_op jit(solution)/shard_map/reduce_scatter | solution.py:322
  880.2 188.6 %reduce-scatter.9.cloned.1.call-done = f32[32,4096]{1,0:T(8,128)} async-done(((f32[1024,4096]{1,0:T(8,128)}), f32[32,4096]{1,0:T(8,128)}) %reduce-scatter.9.cloned.1.call-update) | async-done | bytes 524304 | tf_op jit(solution)/shard_map/reduce_scatter | solution.py:328
  1068.9 187.4 %reduce-scatter.11.cloned.1.call-done = f32[128,1024]{1,0:T(8,128)} async-done(((f32[4096,1024]{1,0:T(8,128)}), f32[128,1024]{1,0:T(8,128)}) %reduce-scatter.11.cloned.1.call-update) | async-done | bytes 524304 | tf_op jit(solution)/shard_map/reduce_scatter | solution.py:330
  (528 shorter events, 223.0 us)
Async XLA Ops:
  7.2 76.2 %all-gather.11.cloned.1.call-start = ((), (), s32[]{:S(2)}) async-start(), calls=%async_computation.8 | async-start | bytes 6488064 | tf_op jit(solution)/shard_map/all_gather | solution.py:79
  7.9 141.0 %all-gather.21.cloned.1.call-start = ((), (), s32[]{:S(2)}) async-start(), calls=%async_computation.17 | async-start | bytes 4718592 | tf_op jit(solution)/shard_map/all_gather | solution.py:134
  58.6 28.8 %copy-start.30 = (f32[128]{0:T(128)}, f32[128]{0:T(128)S(1)}, u32[]{:S(2)}) copy-start(f32[128]{0:T(128)S(1)} %fusion.131) | copy-start | bytes 1540
  87.4 18.3 %copy-start.22 = (s32[7]{0:T(128)S(1)}, s32[7]{0:T(128)}, u32[]{:S(2)}) copy-start(s32[7]{0:T(128)} %param.36) | copy-start | bytes 88
  87.4 18.4 %copy-start.33 = (f32[16]{0:T(128)S(1)}, f32[16]{0:T(128)}, u32[]{:S(2)}) copy-start(f32[16]{0:T(128)} %param.35) | copy-start | bytes 196
  103.7 225.6 %all-gather.13.cloned.1.call-start = ((), (), s32[]{:S(2)}) async-start(), calls=%async_computation.9 | async-start | bytes 2162688 | tf_op jit(solution)/shard_map/all_gather | solution.py:81
  104.4 227.3 %all-gather.15.cloned.1.call-start = ((), (), s32[]{:S(2)}) async-start(), calls=%async_computation.10 | async-start | bytes 8650752 | tf_op jit(solution)/shard_map/all_gather | solution.py:85
  105.0 260.3 %all-gather.17.cloned.1.call-start = ((), (), s32[]{:S(2)}) async-start(), calls=%async_computation.11 | async-start | bytes 8650752 | tf_op jit(solution)/shard_map/all_gather | solution.py:87
  105.8 55.9 %copy-start.15 = (bf16[512,1,1,256]{3,0,1,2:T(8,128)(2,1)}, bf16[512,1,1,256]{3,0,1,2:T(8,128)(2,1)S(1)}, u32[]{:S(2)}) copy-start(bf16[512,1,1,256]{3,0,1,2:T(8,128)(2,1)S(1)} %slice.80) | copy-start | bytes 786436
  174.5 113.2 %copy-start.32 = (bf16[128]{0:T(256)(128)(2,1)S(1)}, bf16[128]{0:T(256)(128)(2,1)}, u32[]{:S(2)}) copy-start(bf16[128]{0:T(256)(128)(2,1)} %param.32) | copy-start | bytes 772
  280.4 7.2 copy-start.24
  280.4 7.3 copy-start.34
  280.4 48.8 %copy-start.2 = (bf16[128,1024]{1,0:T(8,128)(2,1)S(1)}, bf16[128,1024]{1,0:T(8,128)(2,1)}, u32[]{:S(2)}) copy-start(bf16[128,1024]{1,0:T(8,128)(2,1)} %param.22) | copy-start | bytes 786436
  283.9 44.8 %all-to-all-start.1 = ((bf16[4,2,16384]{2,1,0:T(2,128)(2,1)}), bf16[4,2,16384]{2,1,0:T(2,128)(2,1)S(1)}, u32[]{:S(2)}, u32[]{:S(2)}) async-start(bf16[4,2,16384]{2,1,0:T(2,128)(2,1)} %reshape.806), calls=%async_computation.1 | async-start | bytes 524288 | tf_op jit(solution)/shard_map/all_to_all | solution.py:168
  287.5 107.6 %all-gather.23.cloned.1.call-start = ((), (), s32[]{:S(2)}) async-start(), calls=%async_computation.18 | async-start | bytes 2359296 | tf_op jit(solution)/shard_map/all_gather | solution.py:255
  328.7 206.2 %all-gather.19.cloned.1.call-start = ((), (), s32[]{:S(2)}) async-start(), calls=%async_computation.12 | async-start | bytes 2359296 | tf_op jit(solution)/shard_map/all_gather | solution.py:256
  331.7 33.6 %copy-start.12 = (bf16[128,1024]{1,0:T(8,128)(2,1)S(1)}, bf16[128,1024]{1,0:T(8,128)(2,1)}, u32[]{:S(2)}) copy-start(bf16[128,1024]{1,0:T(8,128)(2,1)} %param.37) | copy-start | bytes 786436
  336.5 37.1 %copy-start.3 = (f32[128,4096]{1,0:T(8,128)}, f32[128,4096]{1,0:T(8,128)S(1)}, u32[]{:S(2)}) copy-start(f32[128,4096]{1,0:T(8,128)S(1)} %convolution_add_fusion) | copy-start | bytes 6291460
  365.3 8.3 copy-start.1
  376.6 10.8 copy-start.19
  376.9 46.9 %copy-start.6 = (f32[128,1024]{1,0:T(8,128)}, f32[128,1024]{1,0:T(8,128)S(1)}, u32[]{:S(2)}) copy-start(f32[128,1024]{1,0:T(8,128)S(1)} %get-tuple-element.1133) | copy-start | bytes 1572868
  377.0 46.9 %copy-start.27 = (f32[128]{0:T(128)}, f32[128]{0:T(128)S(1)}, u32[]{:S(2)}) copy-start(f32[128]{0:T(128)S(1)} %negate_multiply_fusion.1) | copy-start | bytes 1540
  387.4 416.4 %reduce-scatter.7.cloned.1.call-start = ((), (), s32[]{:S(2)}) async-start(), calls=%async_computation.14 | async-start | bytes 4325376 | tf_op jit(solution)/shard_map/reduce_scatter | solution.py:324
  402.1 21.7 %copy-start.18 = (bf16[128,4,1,256]{0,3,1,2:T(8,128)(2,1)S(1)}, bf16[128,4,1,256]{0,3,1,2:T(8,128)(2,1)}, u32[]{:S(2)}) copy-start(bf16[128,4,1,256]{0,3,1,2:T(8,128)(2,1)} %copy-done.17) | copy-start | bytes 786436
  426.7 17.2 %copy-start.35 = (s32[8]{0:T(128)S(1)}, s32[8]{0:T(128)}, u32[]{:S(2)}) copy-start(s32[8]{0:T(128)} %copy-done.34) | copy-start | bytes 100
  426.7 453.5 %reduce-scatter.5.cloned.1.call-start = ((), (), s32[]{:S(2)}) async-start(), calls=%async_computation.13 | async-start | bytes 12976128 | tf_op jit(solution)/shard_map/reduce_scatter | solution.py:322
  443.9 5.6 copy-start.25
  460.7 5.6 copy-start.36
  466.3 5.6 copy-start.25
  471.9 5.6 copy-start.36
  477.5 5.6 copy-start.25
  483.1 5.6 copy-start.36
  494.4 5.6 copy-start.36
  500.0 5.6 copy-start.25
  505.6 5.6 copy-start.36
  511.2 5.6 copy-start.25
  516.8 5.6 copy-start.36
  522.5 5.6 copy-start.25
  528.1 5.6 copy-start.36
  541.9 7.0 copy-start.26
  548.9 7.0 copy-start.37
  557.1 5.7 copy-start.20
  567.5 7.0 copy-start.37
  575.7 5.8 copy-start.20
  586.2 7.0 copy-start.37
  594.4 5.8 copy-start.20
  604.9 7.0 copy-start.37
  613.1 5.8 copy-start.20
  623.6 7.0 copy-start.37
  631.8 5.8 copy-start.20
  642.3 7.0 copy-start.37
  650.5 5.8 copy-start.20
  661.1 7.0 copy-start.37
  669.2 5.8 copy-start.20
  679.8 7.0 copy-start.37
  687.9 5.8 copy-start.20
  719.5 6.8 copy-start.10
  719.9 6.4 copy-start.8
  726.3 342.5 %reduce-scatter.9.cloned.1.call-start = ((), (), s32[]{:S(2)}) async-start(), calls=%async_computation.15 | async-start | bytes 17301504 | tf_op jit(solution)/shard_map/reduce_scatter | solution.py:328
  736.5 519.7 %reduce-scatter.11.cloned.1.call-start = ((), (), s32[]{:S(2)}) async-start(), calls=%async_computation.16 | async-start | bytes 17301504 | tf_op jit(solution)/shard_map/reduce_scatter | solution.py:330
  747.2 7.9 slice-start
  747.9 7.0 copy-start.11
  747.9 7.2 slice-start.1
  747.9 7.2 copy-start.9
  (38 other events, 118.7 us)
Sparse Core Ops, SparseCore 0:
  11.0 72.3 all-gather.10
  103.8 45.0 all-gather.20
  151.9 55.1 all-gather.12
  210.0 76.3 all-gather.14
  289.2 76.1 all-gather.16
  367.3 27.6 all-gather.22
  396.7 29.0 all-gather.18
  428.7 142.0 reduce-scatter.6
  726.5 153.7 reduce-scatter.4
  883.1 185.7 reduce-scatter.8
  1071.8 184.3 reduce-scatter.10
where the time goes:
time: 1280 us; the launch traced here: 1260 us
  waiting for transfers between devices  558 us (44%)
  matrix products  286 us (22%)
  blocking collectives  195 us (15%)
  local copies, waits for them, and re-layouts  119 us (9%)
  other arithmetic  69.2 us (5%)
  loops' own time  16.9 us (1%)
  between operations  14.8 us (1%)
    reduce_scatter x1, waiting for transfers between devices, body(): lax.psum_scatter(up_grad, ('ulysses', 'blk'), scatter_dimension=0, tiled=...  189 us
    reduce_scatter x1, waiting for transfers between devices, body(): lax.psum_scatter(down_grad, ('ulysses', 'blk'), scatter_dimension=0, tile...  187 us
    unnamed x2, blocking collectives  82.6 us
    dot_general x24, matrix products, score_block(): jnp.einsum('qhd,khd->hqk', queries, keys, preferred_element_type=jnp.floa...  76.9 us
    reduce_scatter x1, waiting for transfers between devices, body(): lax.psum_scatter(qkv_grad, ('ulysses', 'blk'), scatter_dimension=0, tiled...  76.4 us
    dot_general x8, matrix products, key_step(): jnp.einsum('hqk,qhd->khd', grad_scores, query_block, preferred_element_ty...  46 us
    dot_general x8, matrix products, query_step(): jnp.einsum('hqk,khd->hqd', grad_scores, kv_block[:, 0], preferred_element...  44.8 us
    all_gather x1, waiting for transfers between devices, body(): piece_rows = lax.all_gather(key_value, 'blk', axis=0, tiled=True)  42.9 us
  transfers between devices with their start and end apart: 12, of which 7 were waited for; matrix products, arithmetic and copies ran while one was open for 36% of the time, Pallas kernels for 0%

commit v1 on v0

--- a/solution.py
+++ b/solution.py
@@ -1,7 +1,882 @@
+import functools
+
 import jax
 import jax.numpy as jnp
 from jax import lax
+from jax.experimental import pallas as pl
+from jax.experimental.pallas import tpu as pltpu
 from jax.sharding import PartitionSpec as P
+
+BF = jnp.bfloat16
+F32 = jnp.float32
+MESH = pl.DeviceIdType.MESH
+VMEM_LIMIT = 60 * 2**20
+NT = (((1,), (1,)), ((), ()))
+TN = (((0,), (0,)), ((), ()))
+NN = (((1,), (0,)), ((), ()))
+
+
+def dot(a, b, dims=NN):
+    return lax.dot_general(a, b, dims, preferred_element_type=F32)
+
+
+def flip(index, mask):
+    out = index
+    bit = 1
+    while bit <= mask:
+        if mask & bit:
+            out = out + bit - 2 * bit * ((index // bit) % 2)
+        bit *= 2
+    return out
+
+
+def ds(start, size, align=None):
+    if not isinstance(start, int):
+        start = pl.multiple_of(start, align or size)
+    return pl.ds(start, size)
+
+
+class Wire:
+    def __init__(self, ssem, rsem, lsem=None):
+        self.ssem, self.rsem, self.lsem = ssem, rsem, lsem
+        self.used = 0
+        self.local = 0
+        self.u = lax.axis_index("ulysses")
+        self.b = lax.axis_index("blk")
+        self.sent = []
+
+    def take(self, count):
+        first = self.used
+        self.used += count
+        return first
+
+    def make(self, src, dst, device, at, sent_at=None):
+        return pltpu.make_async_remote_copy(
+            src_ref=src,
+            dst_ref=dst,
+            send_sem=self.ssem.at[at if sent_at is None else sent_at],
+            recv_sem=self.rsem.at[at],
+            device_id=device,
+            device_id_type=MESH,
+        )
+
+    def blk(self, k, src, dst):
+        copy = self.make(src, dst, (self.u, flip(self.b, k)), self.take(1))
+        copy.start()
+        self.sent.append(copy)
+        return copy
+
+    def uly(self, k, src, dst):
+        copy = self.make(src, dst, (flip(self.u, k), self.b), self.take(1))
+        copy.start()
+        self.sent.append(copy)
+        return copy
+
+    def near(self, ku, kb, src, dst):
+        copy = self.make(src, dst, (flip(self.u, ku), flip(self.b, kb)), self.take(1))
+        copy.start()
+        self.sent.append(copy)
+        return copy
+
+    def here(self, src, dst):
+        copy = pltpu.make_async_copy(src, dst, self.lsem.at[self.local])
+        self.local += 1
+        copy.start()
+        return copy
+
+    def finish(self):
+        for copy in self.sent:
+            copy.wait_send()
+
+
+def greet(u, b, blk_masks, uly_masks, both=()):
+    barrier = pltpu.get_barrier_semaphore()
+    for k in blk_masks:
+        pl.semaphore_signal(barrier, inc=1, device_id=(u, flip(b, k)), device_id_type=MESH)
+    for k in uly_masks:
+        pl.semaphore_signal(barrier, inc=1, device_id=(flip(u, k), b), device_id_type=MESH)
+    for ku, kb in both:
+        pl.semaphore_signal(barrier, inc=1, device_id=(flip(u, ku), flip(b, kb)), device_id_type=MESH)
+    pl.semaphore_wait(barrier, len(blk_masks) + len(uly_masks) + len(both))
+
+
+def norm_parts(values):
+    center = jnp.mean(values, axis=-1, keepdims=True)
+    offset = values - center
+    spread = jnp.mean(offset * offset, axis=-1, keepdims=True)
+    inv = lax.rsqrt(spread + 1e-05)
+    return offset * inv, inv
+
+
+def head_mask(shape, head):
+    lane = lax.broadcasted_iota(jnp.int32, shape, len(shape) - 1)
+    return (lane // 64) == head
+
+
+def doc_begin(starts_ref, positions):
+    begin = jnp.zeros_like(positions)
+    for d in range(starts_ref.shape[0]):
+        first = starts_ref[d]
+        begin = jnp.where(positions >= first, jnp.full_like(positions, first), begin)
+    return begin
+
+
+def forward_kernel(
+    tok, wqkv, wproj, wup, wdown, pack, slopes, starts,
+    att_o, q_o, kv_o, lse_o, n1_o, wqkv_o, par_o, wproj_o, wup_o, wdown_o,
+    x_ag, stq, stu, atth, vec, ssem, rsem, lsem,
+):
+    w = Wire(ssem, rsem, lsem)
+    u, b = w.u, w.b
+    z, c, zh = b // 2, b % 2, b // 4
+    x, y = u % 2, u // 2
+    rows = tok.shape[0]
+    group = 8 * rows
+    pair = 2 * rows
+    greet(u, b, range(1, 8), range(1, 4), [(1, k) for k in range(1, 4)])
+
+    par_o[pl.ds(u * 8 + b, 1)] = pack[...][None]
+    p1 = [w.blk(k, pack, par_o.at[u * 8 + b]) for k in range(1, 8)]
+    for r in range(8):
+        for part in range(3):
+            stq[r, :, part * 128:(part + 1) * 128] = wqkv[:, part * 1024 + r * 128:part * 1024 + (r + 1) * 128]
+    wrow = ds((u * 8 + b) * 32, 32)
+    q1 = [w.blk(k, stq.at[flip(b, k)], wqkv_o.at[wrow]) for k in range(1, 8)]
+    wqkv_o[wrow] = stq[b]
+    t_sib = w.blk(1, tok, x_ag.at[ds(b * rows, rows)])
+    t_z = {k: w.blk(2 * k, tok, x_ag.at[ds(b * rows, rows)]) for k in (1, 2, 3)}
+    x_ag[ds(b * rows, rows)] = tok[...]
+    for r in range(8):
+        for ch in range(4):
+            src = ((ch // 2) * 16 + (r // 4) * 8 + (ch % 2) * 4 + r % 4) * 128
+            stu[r, :, ch * 128:(ch + 1) * 128] = wup[:, src:src + 128]
+    rank = x * 4 + b % 4
+    up_row = ds((b % 4) * 32, 32)
+    up_mine = wup_o.at[u, zh, up_row]
+    up1 = [
+        w.near(k // 4, k % 4, stu.at[flip(rank, k)], up_mine) for k in range(1, 8)
+    ]
+    l_up = w.here(stu.at[rank], up_mine)
+    l_down = w.here(wdown, wdown_o.at[y, zh])
+    l_proj = w.here(wproj, wproj_o.at[u, z, c])
+
+    for copy in p1:
+        copy.wait_recv()
+    mine = par_o.at[ds(u * 8, 8)]
+    p2 = [w.uly(k, mine, mine) for k in range(1, 4)]
+    for copy in q1:
+        copy.wait_recv()
+    mine = wqkv_o.at[ds(u * 256, 256)]
+    q2 = [w.uly(k, mine, mine) for k in range(1, 4)]
+    t_sib.wait_recv()
+    t_z[1].wait_recv()
+    fwd = {}
+
+    def to_sibling(k):
+        slot = x_ag.at[ds(flip(b, 2 * k) * rows, rows)]
+        fwd[k] = w.blk(1, slot, slot)
+
+    to_sibling(1)
+    d1 = w.blk(4, wdown, wdown_o.at[y, zh])
+    for copy in up1:
+        copy.wait_recv()
+    l_up.wait()
+    mine = wup_o.at[ds(y * 2, 2), zh]
+    up2 = w.blk(4, mine, mine)
+    pr1 = [w.blk(2 * k, wproj, wproj_o.at[u, z, c]) for k in range(1, 4)]
+
+    for copy in p2:
+        copy.wait_recv()
+    for t in range(8):
+        tiles = [pltpu.roll(par_o[4 * t + k], 32 * k, 1) if k else par_o[4 * t] for k in range(4)]
+        vec[:, t * 128:(t + 1) * 128] = (tiles[0] + tiles[1]) + (tiles[2] + tiles[3])
+    q_bias = (par_o[2 * b] + pltpu.roll(par_o[2 * b + 1], 64, 1))[6:7]
+    v_bias = (par_o[16 + 2 * b] + pltpu.roll(par_o[17 + 2 * b], 64, 1))[6:7]
+    bias = jnp.concatenate([q_bias, jnp.zeros_like(q_bias), v_bias], axis=1)
+
+    def normalize(zc):
+        at = ds(zc * pair, pair)
+        n, _ = norm_parts(x_ag[at].astype(F32))
+        n1_o[at] = (n * vec[0:1] + vec[1:2]).astype(BF)
+
+    halo = w.take(4)
+    hand = []
+
+    def project(zc):
+        at = ds(zc * pair, pair)
+        out = (dot(n1_o[at], wqkv_o[...]) + bias).astype(BF)
+        q_o[at] = out[:, :128]
+        own = ds(group + zc * pair, pair)
+        kv_o[own] = out[:, 128:]
+        copy = w.make(kv_o.at[own], kv_o.at[at], (jnp.minimum(u + 1, 3), b), halo + zc)
+
+        @pl.when(u < 3)
+        def _():
+            copy.start()
+
+        hand.append(copy)
+
+    normalize(z)
+    t_z[2].wait_recv()
+    to_sibling(2)
+    fwd[1].wait_recv()
+    normalize(flip(z, 1))
+    for copy in q2:
+        copy.wait_recv()
+    project(z)
+    project(flip(z, 1))
+    t_z[3].wait_recv()
+    to_sibling(3)
+    for k in (2, 3):
+        fwd[k].wait_recv()
+        normalize(flip(z, k))
+        project(flip(z, k))
+    d1.wait_recv()
+    l_down.wait()
+    mine = wdown_o.at[y]
+    d2 = w.uly(2, mine, mine)
+    up2.wait_recv()
+    mine = wup_o.at[ds(y * 2, 2)]
+    up3 = w.uly(2, mine, mine)
+    for copy in pr1:
+        copy.wait_recv()
+    l_proj.wait()
+    mine = wproj_o.at[u, :, c]
+    pr2 = [w.uly(k, mine, mine) for k in range(1, 4)]
+
+    @pl.when(u == 0)
+    def _():
+        kv_o[0:group] = jnp.zeros((group, 256), BF)
+
+    window = group + pair
+    krow = lax.broadcasted_iota(jnp.int32, (window, pair), 0)
+    qcol = lax.broadcasted_iota(jnp.int32, (window, pair), 1)
+    causal = krow - group <= qcol
+    kslope = (krow[:, :1] - group).astype(F32)
+    att_at = w.take(8)
+    lanes = ds(b * 128, 128)
+
+    def attend(step, carry):
+        i = 3 - step
+
+        @pl.when(u > 0)
+        def _():
+            w.make(
+                kv_o.at[ds(i * pair, pair)], kv_o.at[ds(i * pair, pair)], (u, b), halo + i
+            ).wait_recv()
+
+        qpos = lax.broadcasted_iota(jnp.int32, (1, pair), 1) + i * pair
+        begin = doc_begin(starts, qpos + u * group) - u * group - i * pair + group
+        allowed = causal & (krow >= begin)
+        span = ds(i * pair, window, pair)
+        keys = kv_o[span, 0:128]
+        vals = kv_o[span, 128:256]
+        at = ds(i * pair, pair)
+        query = q_o[at]
+        out = None
+        for h in range(2):
+            qh = jnp.where(head_mask((pair, 128), h), query, jnp.zeros_like(query))
+            s = dot(keys, qh, NT) * 0.125 + slopes[2 * b + h] * kslope
+            s = jnp.where(allowed, s, -1e30)
+            top = jnp.max(s, axis=0, keepdims=True)
+            p = jnp.exp(s - top)
+            total = jnp.sum(p, axis=0, keepdims=True)
+            lse_o[h:h + 1, at] = top + jnp.log(total)
+            o = dot(vals, p.astype(BF), TN) * (1.0 / total)
+            if h == 0:
+                out = o
+            else:
+                out = jnp.where(lax.broadcasted_iota(jnp.int32, o.shape, 0) < 64, out, o)
+        atth[at] = out.T.astype(BF)
+        for half in range(2):
+            target = 2 * i + half
+            piece = atth.at[ds(target * rows, rows)]
+
+            @pl.when(target != b)
+            def _():
+                w.make(piece, att_o.at[:, lanes], (u, target), att_at + b, att_at + target).start()
+
+        return carry
+
+    lax.fori_loop(0, 4, attend, 0)
+    att_o[:, lanes] = atth[ds(b * rows, rows)]
+
+    for copy in pr2:
+        copy.wait_recv()
+    mine = wproj_o.at[:, :, c]
+    pr3 = w.blk(1, mine, mine)
+    for k in range(1, 8):
+        other = flip(b, k)
+        w.make(
+            atth.at[ds(other * rows, rows)], att_o.at[:, ds(other * 128, 128)], (u, other), att_at + other
+        ).wait_recv()
+        w.make(
+            atth.at[ds(other * rows, rows)], att_o.at[:, lanes], (u, other), att_at + b, att_at + other
+        ).wait_send()
+    up3.wait_recv()
+    d2.wait_recv()
+    pr3.wait_recv()
+
+    @pl.when(u < 3)
+    def _():
+        for copy in hand:
+            copy.wait_send()
+
+    w.finish()
+
+
+def forward_call(tok, wqkv, wproj, wup, wdown, pack, slopes, starts):
+    rows = tok.shape[0]
+    group = 8 * rows
+    v = pl.BlockSpec(memory_space=pltpu.VMEM)
+    s = pl.BlockSpec(memory_space=pltpu.SMEM)
+    a = pl.BlockSpec(memory_space=pl.ANY)
+    sds = jax.ShapeDtypeStruct
+    return pl.pallas_call(
+        forward_kernel,
+        name="forward_attention",
+        out_shape=(
+            sds((rows, 1024), BF),
+            sds((group, 128), BF),
+            sds((2 * group, 256), BF),
+            sds((2, group), F32),
+            sds((group, 1024), BF),
+            sds((1024, 384), BF),
+            sds((32, 8, 128), F32),
+            sds((4, 4, 2, 32, 1024), BF),
+            sds((4, 2, 128, 512), BF),
+            sds((2, 2, rows, 1024), BF),
+        ),
+        in_specs=[v, v, a, v, a, v, s, s],
+        out_specs=(v, v, v, v, v, v, v, a, a, a),
+        scratch_shapes=[
+            pltpu.VMEM((group, 1024), BF),
+            pltpu.VMEM((8, 32, 384), BF),
+            pltpu.VMEM((8, 32, 512), BF),
+            pltpu.VMEM((group, 128), BF),
+            pltpu.VMEM((8, 1024), F32),
+            pltpu.SemaphoreType.DMA((64,)),
+            pltpu.SemaphoreType.DMA((64,)),
+            pltpu.SemaphoreType.DMA((4,)),
+        ],
+        compiler_params=pltpu.CompilerParams(
+            collective_id=0, has_side_effects=True, vmem_limit_bytes=VMEM_LIMIT
+        ),
+    )(tok, wqkv, wproj, wup, wdown, pack, slopes, starts)
+
+
+def pack_vectors(*vectors):
+    parts = []
+    for v in vectors:
+        parts.append(v)
+        if v.shape[0] < 128:
+            parts.append(jnp.zeros((128 - v.shape[0],), v.dtype))
+    return jnp.concatenate(parts).reshape(8, 128).astype(F32)
+
+
+def mlp_kernel(
+    tok, att, wproj, wup, wdown, cot, par,
+    out_o, gmix_o, gbr_o, gatt_o, gdown_o, gup_o, small_o, upb_o,
+    n_all, c_all, act_all, gup_all, p_out, p_g, s_out, s_g, z_out, z_g, keep_out, keep_g, vec, ssem, rsem,
+):
+    w = Wire(ssem, rsem)
+    u, b = w.u, w.b
+    x, c = u % 2, b % 2
+    rows = tok.shape[0]
+    pair = 2 * rows
+    rank = x * 4 + b % 4
+    hops = ((0, 2), (1, 0), (1, 2))
+    greet(u, b, (), (), [(k // 4, k % 4) for k in range(1, 8)])
+
+    def gather(src, buf):
+        slot = buf.at[ds(rank * rows, rows)]
+        sib = w.blk(1, src, slot)
+        return sib, [w.near(ku, kb, src, slot) for ku, kb in hops]
+
+    def pass_on(copies, buf, i):
+        ku, kb = hops[i]
+        copies[i].wait_recv()
+        slot = buf.at[ds(flip(rank, ku * 4 + kb) * rows, rows)]
+        return w.blk(1, slot, slot)
+
+    c_sib, c_far = gather(cot, c_all)
+    c_all[ds(rank * rows, rows)] = cot[...]
+    for t in range(8):
+        tiles = [pltpu.roll(par[4 * t + k], 32 * k, 1) if k else par[4 * t] for k in range(4)]
+        vec[:, t * 128:(t + 1) * 128] = (tiles[0] + tiles[1]) + (tiles[2] + tiles[3])
+    up_bias = jnp.concatenate(
+        [par[(ch // 2) * 16 + x * 8 + (ch % 2) * 4 + b % 4][7:8] for ch in range(4)], axis=1
+    )
+    mixed = tok[...].astype(F32) + dot(att[...], wproj[...]) + vec[2:3]
+    n2, inv2 = norm_parts(mixed)
+    n_all[ds(rank * rows, rows)] = (n2 * vec[3:4] + vec[4:5]).astype(BF)
+    n_sib, n_far = gather(n_all.at[ds(rank * rows, rows)], n_all)
+    c_fwd = [pass_on(c_far, c_all, i) for i in range(3)]
+    cot_f = cot[...].astype(F32)
+    small_o[0:1] = jnp.sum(cot_f, axis=0, keepdims=True)
+
+    def forward(chip):
+        at = ds(chip * pair, pair)
+        up = dot(n_all[at], wup[...]) + up_bias
+        square = up * up
+        th = jnp.tanh(0.7978845608028654 * (up + 0.044715 * square * up))
+        act = (0.5 * up * (1.0 + th)).astype(BF)
+        slope = 0.5 * (1.0 + th) + 0.5 * up * (1.0 - th * th) * (
+            0.7978845608028654 * (1.0 + 3.0 * 0.044715 * square)
+        )
+        gup = (dot(c_all[at], wdown[...], NT) * slope).astype(BF)
+        act_all[at] = act
+        gup_all[at] = gup
+        p_out[at] = dot(act, wdown[...]).astype(BF)
+        p_g[at] = dot(gup, wup[...], NT).astype(BF)
+
+    def swap(chip, i):
+        other = ds(chip * pair + (1 - c) * rows, rows)
+        return (w.blk(1, p_g.at[other], s_g.at[i]), w.blk(1, p_out.at[other], s_out.at[i]))
+
+    chip = rank // 2
+    c_sib.wait_recv()
+    n_sib.wait_recv()
+    forward(chip)
+    swaps = [swap(chip, 3)]
+    sends = []
+
+    def merge(i):
+        ku, kb = hops[i]
+        far = flip(chip, (ku * 4 + kb) // 2)
+        own = ds(far * pair + c * rows, rows)
+        for copy in swaps[i + 1]:
+            copy.wait_recv()
+        keep_g[i] = (p_g[own].astype(F32) + s_g[i].astype(F32)).astype(BF)
+        first = w.near(ku, kb, keep_g.at[i], z_g.at[i])
+        keep_out[i] = (p_out[own].astype(F32) + s_out[i].astype(F32)).astype(BF)
+        sends.append((first, w.near(ku, kb, keep_out.at[i], z_out.at[i])))
+
+    n_fwd = [None] * 3
+    n_fwd[0] = pass_on(n_far, n_all, 0)
+    for i in range(3):
+        if i < 2:
+            n_fwd[i + 1] = pass_on(n_far, n_all, i + 1)
+        c_fwd[i].wait_recv()
+        n_fwd[i].wait_recv()
+        ku, kb = hops[i]
+        far = flip(chip, (ku * 4 + kb) // 2)
+        forward(far)
+        swaps.append(swap(far, i))
+        if i > 0:
+            merge(i - 1)
+    merge(2)
+    half = act_all.shape[1] // 2
+    for j in range(2):
+        span = slice(j * half, (j + 1) * half)
+        gdown_o[span] = dot(act_all[:, span], c_all[...], TN).astype(BF)
+        gup_o[:, span] = dot(n_all[...], gup_all[:, span], TN).astype(BF)
+    upb_o[...] = jnp.sum(gup_all[...].astype(F32), axis=0, keepdims=True)
+
+    own = ds(chip * pair + c * rows, rows)
+    for copy in swaps[0]:
+        copy.wait_recv()
+    g = p_g[own].astype(F32) + s_g[3].astype(F32)
+    for i in range(3):
+        sends[i][0].wait_recv()
+        g = g + z_g[i].astype(F32)
+    small_o[1:2] = jnp.sum(g * n2, axis=0, keepdims=True)
+    small_o[2:3] = jnp.sum(g, axis=0, keepdims=True)
+    e = g * vec[3:4]
+    gmix = cot_f + inv2 * (
+        e - jnp.mean(e, axis=-1, keepdims=True) - n2 * jnp.mean(e * n2, axis=-1, keepdims=True)
+    )
+    gmix_o[...] = gmix
+    small_o[3:4] = jnp.sum(gmix, axis=0, keepdims=True)
+    gbr = gmix.astype(BF)
+    gbr_o[...] = gbr
+    gatt_o[...] = dot(gbr, wproj[...], NT).astype(BF)
+    out = mixed + vec[5:6] + p_out[own].astype(F32) + s_out[3].astype(F32)
+    for i in range(3):
+        sends[i][1].wait_recv()
+        out = out + z_out[i].astype(F32)
+    out_o[...] = out.astype(BF)
+    w.finish()
+
+
+def mlp_call(tok, att, wproj, wup, wdown, cot, par):
+    rows = tok.shape[0]
+    group = 8 * rows
+    width = tok.shape[1]
+    hidden = wup.shape[1]
+    v = pl.BlockSpec(memory_space=pltpu.VMEM)
+    sds = jax.ShapeDtypeStruct
+    return pl.pallas_call(
+        mlp_kernel,
+        name="feed_forward",
+        out_shape=(
+            sds((rows, width), BF),
+            sds((rows, width), F32),
+            sds((rows, width), BF),
+            sds((rows, width), BF),
+            sds((hidden, width), BF),
+            sds((width, hidden), BF),
+            sds((4, width), F32),
+            sds((1, hidden), F32),
+        ),
+        in_specs=[v] * 7,
+        out_specs=(v,) * 8,
+        scratch_shapes=[
+            pltpu.VMEM((group, width), BF),
+            pltpu.VMEM((group, width), BF),
+            pltpu.VMEM((group, hidden), BF),
+            pltpu.VMEM((group, hidden), BF),
+            pltpu.VMEM((group, width), BF),
+            pltpu.VMEM((group, width), BF),
+            pltpu.VMEM((4, rows, width), BF),
+            pltpu.VMEM((4, rows, width), BF),
+            pltpu.VMEM((3, rows, width), BF),
+            pltpu.VMEM((3, rows, width), BF),
+            pltpu.VMEM((3, rows, width), BF),
+            pltpu.VMEM((3, rows, width), BF),
+            pltpu.VMEM((8, width), F32),
+            pltpu.SemaphoreType.DMA((40,)),
+            pltpu.SemaphoreType.DMA((40,)),
+        ],
+        compiler_params=pltpu.CompilerParams(
+            collective_id=1, has_side_effects=True, vmem_limit_bytes=VMEM_LIMIT
+        ),
+    )(tok, att, wproj, wup, wdown, cot, par)
+
+
+def backward_kernel(
+    tok, gatt, q, kv, lse, n1, wqkv, gmix, gbr, att, gdown, gup, small, upb, par, slopes, starts,
+    in_o, down_o, up_o, qkv_o, proj_o, vec_o,
+    gh, dkv, halo_b, gqkv, pieces, p_g, s_g, keep_g, z_g,
+    r_down, r_up, k_down, k_up, f_down, f_up, m_up, a_up,
+    p_proj, s_proj, k_proj, r_proj, m_proj, a_proj,
+    p_qkv, r_qkv, m_qkv, a_qkv,
+    sm, sm_r, sm_k, sm_a, vec, ssem, rsem,
+):
+    w = Wire(ssem, rsem)
+    u, b = w.u, w.b
+    z, c, zh = b // 2, b % 2, b // 4
+    x, y = u % 2, u // 2
+    rows = tok.shape[0]
+    group = 8 * rows
+    pair = 2 * rows
+    rank = x * 4 + b % 4
+    greet(u, b, range(1, 8), range(1, 4), [(1, k) for k in range(1, 4)])
+
+    g_to = w.take(8)
+    g_sent = []
+    for k in range(1, 8):
+        other = flip(b, k)
+        copy = w.make(
+            gatt.at[:, ds(other * 128, 128)], gh.at[ds(b * rows, rows)], (u, other), g_to + b, g_to + other
+        )
+        copy.start()
+        g_sent.append(copy)
+    gh[ds(b * rows, rows)] = gatt[:, ds(b * 128, 128)]
+    y1 = w.uly(2, gdown.at[1 - y], r_down)
+    y2 = w.uly(2, gup.at[ds((1 - y) * 2, 2)], r_up)
+    for j in range(4):
+        p_proj[j] = dot(att[:, j * 256:(j + 1) * 256], gbr[...], TN).astype(BF).reshape(4, 2, 32, 1024)
+    pr1 = w.blk(1, p_proj.at[:, :, 1 - c], s_proj)
+    for t in range(8):
+        tiles = [pltpu.roll(par[4 * t + k], 32 * k, 1) if k else par[4 * t] for k in range(4)]
+        vec[:, t * 128:(t + 1) * 128] = (tiles[0] + tiles[1]) + (tiles[2] + tiles[3])
+
+    window = group + pair
+    krow = lax.broadcasted_iota(jnp.int32, (window, pair), 0)
+    qcol = lax.broadcasted_iota(jnp.int32, (window, pair), 1)
+    causal = krow - group <= qcol
+    kslope = (krow[:, :1] - group).astype(F32)
+    dkv[...] = jnp.zeros_like(dkv)
+    halo = w.take(4)
+
+    def hand_back(i):
+        at = ds(i * pair, pair)
+        return w.make(
+            pieces.at[at], halo_b.at[at], (jnp.maximum(u - 1, 0), b), halo + i
+        )
+
+    def attend(i):
+        for half in range(2):
+            source = 2 * i + half
+
+            @pl.when(source != b)
+            def _():
+                w.make(
+                    gatt.at[:, ds(b * 128, 128)], gh.at[ds(source * rows, rows)], (u, b), g_to + source
+                ).wait_recv()
+
+        qpos = lax.broadcasted_iota(jnp.int32, (1, pair), 1) + i * pair
+        begin = doc_begin(starts, qpos + u * group) - u * group - i * pair + group
+        allowed = causal & (krow >= begin)
+        span = slice(i * pair, i * pair + window)
+        at = slice(i * pair, (i + 1) * pair)
+        keys = kv[span, 0:128]
+        vals = kv[span, 128:256]
+        query = q[at]
+        grads = gh[at]
+        dk = dv = dq = None
+        for h in range(2):
+            mask = head_mask((pair, 128), h)
+            qh = jnp.where(mask, query, jnp.zeros_like(query))
+            gr = jnp.where(mask, grads, jnp.zeros_like(grads))
+            s = dot(keys, qh, NT) * 0.125 + slopes[2 * b + h] * kslope
+            p = jnp.where(allowed, jnp.exp(s - lse[h:h + 1, at]), 0.0)
+            dp = dot(vals, gr, NT)
+            delta = jnp.sum(p * dp, axis=0, keepdims=True)
+            gs = (p * (dp - delta)).astype(BF)
+            dv_h = dot(p.astype(BF), gr)
+            dk_h = dot(gs, qh)
+            dq_h = dot(keys, gs, TN)
+            if h == 0:
+                dk, dv, dq = dk_h, dv_h, dq_h
+            else:
+                dk, dv = dk + dk_h, dv + dv_h
+                dq = jnp.where(lax.broadcasted_iota(jnp.int32, dq.shape, 0) < 64, dq, dq_h)
+        gqkv[at, 0:128] = (dq.T * 0.125).astype(BF)
+        dkv[span, 0:128] += dk
+        dkv[span, 128:256] += dv
+        pieces[at] = dkv[at].astype(BF)
+
+        @pl.when(u > 0)
+        def _():
+            hand_back(i).start()
+
+    attend(0)
+    attend(1)
+    pr1.wait_recv()
+    k_proj[...] = (p_proj[:, :, c].astype(F32) + s_proj[...].astype(F32)).astype(BF)
+    pr2 = [w.uly(k, k_proj.at[flip(u, k)], r_proj.at[k - 1]) for k in range(1, 4)]
+    attend(2)
+    attend(3)
+    y1.wait_recv()
+    k_down[...] = (gdown[y].astype(F32) + r_down[...].astype(F32)).astype(BF)
+    z1 = w.blk(4, k_down.at[1 - zh], f_down)
+    y2.wait_recv()
+    k_up[...] = (gup[ds(y * 2, 2)].astype(F32) + r_up[...].astype(F32)).astype(BF)
+    z2 = w.blk(4, k_up.at[:, 1 - zh], f_up)
+
+    for i in range(4):
+        at = slice(i * pair, (i + 1) * pair)
+        own = slice(group + i * pair, group + (i + 1) * pair)
+
+        @pl.when(u < 3)
+        def _():
+            w.make(pieces.at[at], halo_b.at[at], (u, b), halo + i).wait_recv()
+            dkv[own] += halo_b[at].astype(F32)
+
+        gqkv[at, 128:256] = (dkv[own, 0:128] * 0.125).astype(BF)
+        gqkv[at, 256:384] = dkv[own, 128:256].astype(BF)
+
+    swaps = {}
+
+    def spread(k):
+        chip = flip(z, k)
+        at = ds(chip * pair, pair)
+        p_g[at] = dot(gqkv[at], wqkv[...], NT).astype(BF)
+        other = ds(chip * pair + (1 - c) * rows, rows)
+        swaps[k] = w.blk(1, p_g.at[other], s_g.at[k])
+
+    sends = {}
+
+    def merge(k):
+        own = ds(flip(z, k) * pair + c * rows, rows)
+        swaps[k].wait_recv()
+        keep_g[k - 1] = (p_g[own].astype(F32) + s_g[k].astype(F32)).astype(BF)
+        sends[k] = w.blk(2 * k, keep_g.at[k - 1], z_g.at[k - 1])
+
+    spread(3)
+    spread(2)
+    merge(3)
+    spread(1)
+    merge(2)
+    spread(0)
+    merge(1)
+    p_qkv[...] = dot(n1[...], gqkv[...], TN).astype(BF)
+    q2 = [w.uly(k, p_qkv.at[ds(flip(u, k) * 256, 256)], r_qkv.at[k - 1]) for k in range(1, 4)]
+    g_sums = jnp.sum(gqkv[...].astype(F32), axis=0, keepdims=True)
+
+    for copy in pr2:
+        copy.wait_recv()
+    m_proj[...] = (
+        k_proj[u].astype(F32) + r_proj[0].astype(F32) + r_proj[1].astype(F32) + r_proj[2].astype(F32)
+    ).astype(BF)
+    pr3 = [w.blk(2 * k, m_proj.at[flip(z, k)], a_proj.at[k - 1]) for k in range(1, 4)]
+    z1.wait_recv()
+    down_o[...] = (gdown[y, zh].astype(F32) + r_down[zh].astype(F32)) + f_down[...].astype(F32)
+    z2.wait_recv()
+    m_up[...] = (
+        (gup[ds(y * 2, 2), zh].astype(F32) + r_up[:, zh].astype(F32)) + f_up[...].astype(F32)
+    ).astype(BF).reshape(8, 32, 512)
+    up3 = [w.near(k // 4, k % 4, m_up.at[flip(rank, k)], a_up.at[rank]) for k in range(1, 8)]
+    a_up[rank] = m_up[rank]
+
+    own = ds(b * rows, rows)
+    swaps[0].wait_recv()
+    g = p_g[own].astype(F32) + s_g[0].astype(F32)
+    n, inv = norm_parts(tok[...].astype(F32))
+    for k in (1, 2, 3):
+        sends[k].wait_recv()
+        g = g + z_g[k - 1].astype(F32)
+    e = g * vec[0:1]
+    in_o[...] = (
+        gmix[...]
+        + inv * (e - jnp.mean(e, axis=-1, keepdims=True) - n * jnp.mean(e * n, axis=-1, keepdims=True))
+    ).astype(BF)
+    lines = jnp.concatenate(
+        [
+            jnp.sum(g * n, axis=0, keepdims=True), jnp.sum(g, axis=0, keepdims=True),
+            small[3:4], small[1:2], small[2:3], small[0:1], jnp.zeros((2, 1024), F32),
+        ],
+        axis=0,
+    )
+    for d in range(32):
+        sm[d] = lines[:, (d // 4) * 128:(d // 4 + 1) * 128]
+    for at, line in ((2 * b, g_sums[:, 0:128]), (16 + 2 * b, g_sums[:, 256:384])):
+        sm[at, 6:7] = line
+        sm[at + 1, 6:7] = line
+    for ch in range(4):
+        sm[(ch // 2) * 16 + x * 8 + (ch % 2) * 4 + b % 4, 7:8] = upb[:, ch * 128:(ch + 1) * 128]
+    s1 = [w.uly(k, sm.at[ds(flip(u, k) * 8, 8)], sm_r.at[k - 1]) for k in range(1, 4)]
+
+    for copy in q2:
+        copy.wait_recv()
+    m_qkv[...] = (
+        (p_qkv[ds(u * 256, 256)].astype(F32) + r_qkv[0].astype(F32))
+        + (r_qkv[1].astype(F32) + r_qkv[2].astype(F32))
+    ).astype(BF).reshape(8, 32, 384)
+    q3 = [w.blk(k, m_qkv.at[flip(b, k)], a_qkv.at[b]) for k in range(1, 8)]
+    a_qkv[b] = m_qkv[b]
+    for copy in s1:
+        copy.wait_recv()
+    sm_k[...] = (sm[ds(u * 8, 8)] + sm_r[0]) + (sm_r[1] + sm_r[2])
+    s2 = [w.blk(k, sm_k.at[flip(b, k)], sm_a.at[k - 1]) for k in range(1, 8)]
+
+    for copy in pr3:
+        copy.wait_recv()
+    proj_o[...] = (m_proj[z].astype(F32) + a_proj[0].astype(F32)) + (
+        a_proj[1].astype(F32) + a_proj[2].astype(F32)
+    )
+    for copy in up3:
+        copy.wait_recv()
+    for r in range(8):
+        for ch in range(4):
+            to = ((ch // 2) * 16 + (r // 4) * 8 + (ch % 2) * 4 + r % 4) * 128
+            up_o[:, to:to + 128] = a_up[r, :, ch * 128:(ch + 1) * 128].astype(F32)
+    for copy in q3:
+        copy.wait_recv()
+    for r in range(8):
+        for part in range(3):
+            qkv_o[:, part * 1024 + r * 128:part * 1024 + (r + 1) * 128] = a_qkv[
+                r, :, part * 128:(part + 1) * 128
+            ].astype(F32)
+    for copy in s2:
+        copy.wait_recv()
+    total = sm_k[b]
+    for k in range(7):
+        total = total + sm_a[k]
+    line = lax.broadcasted_iota(jnp.int32, (8, 128), 0)
+    by32 = pltpu.roll(total, (128 - 32 * (b % 4)) % 128, 1)
+    by64 = pltpu.roll(total, (128 - 64 * (b % 2)) % 128, 1)
+    vec_o[...] = jnp.where(line < 6, by32, jnp.where(line == 6, by64, total))
+    for copy in g_sent:
+        copy.wait_send()
+
+    @pl.when(u > 0)
+    def _():
+        for i in range(4):
+            hand_back(i).wait_send()
+
+    w.finish()
+
+
+def backward_call(tok, gatt, q, kv, lse, n1, wqkv, gmix, gbr, att, gdown, gup, small, upb, par, slopes, starts):
+    rows, width = tok.shape
+    group = 8 * rows
+    v = pl.BlockSpec(memory_space=pltpu.VMEM)
+    s = pl.BlockSpec(memory_space=pltpu.SMEM)
+    sds = jax.ShapeDtypeStruct
+    vm = pltpu.VMEM
+    return pl.pallas_call(
+        backward_kernel,
+        name="backward_attention",
+        out_shape=(
+            sds((rows, width), BF),
+            sds((rows, width), F32),
+            sds((32, 4096), F32),
+            sds((32, 3072), F32),
+            sds((32, width), F32),
+            sds((8, 128), F32),
+        ),
+        in_specs=[v] * 15 + [s, s],
+        out_specs=(v,) * 6,
+        scratch_shapes=[
+            vm((group, 128), BF),
+            vm((2 * group, 256), F32),
+            vm((group, 256), BF),
+            vm((group, 384), BF),
+            vm((group, 256), BF),
+            vm((group, width), BF),
+            vm((4, rows, width), BF),
+            vm((3, rows, width), BF),
+            vm((3, rows, width), BF),
+            vm((2, rows, width), BF),
+            vm((2, 2, 128, 512), BF),
+            vm((2, rows, width), BF),
+            vm((2, 2, 128, 512), BF),
+            vm((rows, width), BF),
+            vm((2, 128, 512), BF),
+            vm((8, 32, 512), BF),
+            vm((8, 32, 512), BF),
+            vm((4, 4, 2, 32, width), BF),
+            vm((4, 4, 32, width), BF),
+            vm((4, 4, 32, width), BF),
+            vm((3, 4, 32, width), BF),
+            vm((4, 32, width), BF),
+            vm((3, 32, width), BF),
+            vm((1024, 384), BF),
+            vm((3, 256, 384), BF),
+            vm((8, 32, 384), BF),
+            vm((8, 32, 384), BF),
+            vm((32, 8, 128), F32),
+            vm((3, 8, 8, 128), F32),
+            vm((8, 8, 128), F32),
+            vm((7, 8, 128), F32),
+            vm((8, width), F32),
+            pltpu.SemaphoreType.DMA((72,)),
+            pltpu.SemaphoreType.DMA((72,)),
+        ],
+        compiler_params=pltpu.CompilerParams(
+            collective_id=2, has_side_effects=True, vmem_limit_bytes=VMEM_LIMIT
+        ),
+    )(tok, gatt, q, kv, lse, n1, wqkv, gmix, gbr, att, gdown, gup, small, upb, par, slopes, starts)
+
+
+def fast_body(
+    tokens, ln1_gain, ln1_bias, qkv_weight, qv_bias, proj_weight, proj_bias, ln2_gain, ln2_bias,
+    up_weight, up_bias, down_weight, down_bias, alibi_slopes, doc_starts, cotangent,
+):
+    rows, width = tokens.shape
+    pack = pack_vectors(
+        ln1_gain, ln1_bias, proj_bias, ln2_gain, ln2_bias, down_bias, qv_bias, up_bias
+    )
+    att, q, kv, lse, n1, wqkv, par, wproj, wup, wdown = forward_call(
+        tokens, qkv_weight, proj_weight, up_weight, down_weight, pack, alibi_slopes, doc_starts
+    )
+    output, gmix, gbr, gatt, gdown, gup, small, upb = mlp_call(
+        tokens, att, wproj.reshape(width, width), wup.reshape(width, 512), wdown.reshape(512, width),
+        cotangent, par,
+    )
+    grad_in, gd, gu, gq, gp, vec = backward_call(
+        tokens, gatt, q, kv, lse, n1, wqkv, gmix, gbr, att,
+        gdown.reshape(2, 2, rows, width), gup.reshape(4, 2, 128, 512), small, upb, par,
+        alibi_slopes, doc_starts,
+    )
+    return (
+        output, grad_in, vec[0, :32], vec[1, :32], gq, vec[6, :64], gp, vec[2, :32],
+        vec[3, :32], vec[4, :32], gu, vec[7], gd, vec[5, :32],
+    )
+
 
 HEADS = 16
 HEAD_DIM = 64
@@ -47,7 +922,7 @@
     return (jnp.where(allowed[None], raw_scores, -1e30), allowed[None])
 
 
-def body(
+def general_body(
     tokens,
     ln1_gain,
     ln1_bias,
@@ -348,39 +1223,22 @@
     )
 
 
+TOKEN_ROWS = P(("ulysses", "blk"), None)
+VECTOR = P(("ulysses", "blk"))
+
+
 def solution(mesh):
+    whole = P()
     in_specs = (
-        P(("ulysses", "blk"), None),
-        P(("ulysses", "blk")),
-        P(("ulysses", "blk")),
-        P(("ulysses", "blk"), None),
-        P(("ulysses", "blk")),
-        P(("ulysses", "blk"), None),
-        P(("ulysses", "blk")),
-        P(("ulysses", "blk")),
-        P(("ulysses", "blk")),
-        P(("ulysses", "blk"), None),
-        P(("ulysses", "blk")),
-        P(("ulysses", "blk"), None),
-        P(("ulysses", "blk")),
-        P(),
-        P(),
-        P(("ulysses", "blk"), None),
+        TOKEN_ROWS, VECTOR, VECTOR, TOKEN_ROWS, VECTOR, TOKEN_ROWS, VECTOR, VECTOR, VECTOR, TOKEN_ROWS,
+        VECTOR, TOKEN_ROWS, VECTOR, whole, whole, TOKEN_ROWS,
     )
     out_specs = (
-        P(("ulysses", "blk"), None),
-        P(("ulysses", "blk"), None),
-        P(("ulysses", "blk")),
-        P(("ulysses", "blk")),
-        P(("ulysses", "blk"), None),
-        P(("ulysses", "blk")),
-        P(("ulysses", "blk"), None),
-        P(("ulysses", "blk")),
-        P(("ulysses", "blk")),
-        P(("ulysses", "blk")),
-        P(("ulysses", "blk"), None),
-        P(("ulysses", "blk")),
-        P(("ulysses", "blk"), None),
-        P(("ulysses", "blk")),
-    )
-    return jax.shard_map(body, mesh=mesh, in_specs=in_specs, out_specs=out_specs, check_vma=False)
+        TOKEN_ROWS, TOKEN_ROWS, VECTOR, VECTOR, TOKEN_ROWS, VECTOR, TOKEN_ROWS, VECTOR, VECTOR, VECTOR,
+        TOKEN_ROWS, VECTOR, TOKEN_ROWS, VECTOR,
+    )
+    fits = mesh.shape["ulysses"] == 4 and mesh.shape["blk"] == 8
+    return jax.shard_map(
+        fast_body if fits else general_body,
+        mesh=mesh, in_specs=in_specs, out_specs=out_specs, check_vma=False,
+    )

time: 1280 us -> 271 us (0.21); the launches traced: 1260 us -> 270 us
  waiting for transfers between devices: 558 us -> 0 us
  matrix products: 286 us -> 0 us
  Pallas kernels: 0 us -> 252 us
  blocking collectives: 195 us -> 0 us
  local copies, waits for them, and re-layouts: 119 us -> 16.6 us
  other arithmetic: 69.2 us -> 0.6 us
  loops' own time: 16.9 us -> 0 us
  between operations: 14.8 us -> 0.71 us
    reduce_scatter x4 -> x0, waiting for transfers between devices: 452 us -> none  [the longest x1 189 us: body(): lax.psum_scatter(up_grad, ('ulysses', 'blk'), scatter_dimension=0, tiled=...]
    dot_general x68 -> x0, matrix products: 286 us -> none  [the longest x24 76.9 us: score_block(): jnp.einsum('qhd,khd->hqk', queries, keys, preferred_element_type=jnp.floa...]
    pallas_call x0 -> x3, Pallas kernels: none -> 252 us  [the longest x1 98.2 us: forward_call(): pl.pallas_call(forward_kernel, name='forward_attention', out_shape=(sds((...]
    all_gather x7 -> x0, waiting for transfers between devices: 103 us -> none  [the longest x1 42.9 us: body(): piece_rows = lax.all_gather(key_value, 'blk', axis=0, tiled=True)]
    unnamed x2 -> x0, blocking collectives: 82.6 us -> none
    all_gather x3 -> x0, blocking collectives: 70.3 us -> none  [the longest x1 40.9 us: body(): lax.all_gather(up_bias, ('ulysses', 'blk'), axis=0, tiled=True)]
    all_to_all x3 -> x0, blocking collectives: 41.9 us -> none  [the longest x1 18 us: body(): lax.all_to_all(grad_pack.reshape(head_rows, 3, 1, features), 'ulysses', s...]
    reduce_sum x41 -> x0, other arithmetic: 37.4 us -> none  [the longest x8 29.8 us: online_step(): norm_sum = norm_sum * shrink + jnp.sum(weights, axis=-1)]
  transfers between devices with their start and end apart: 12 -> 0, of which waited for: 7 -> 0; matrix products, arithmetic and copies ran while one was open for 36% -> 0% of each run, Pallas kernels for 0% -> 0%
where the time goes in v1:
time: 271 us; the launch traced here: 270 us
  Pallas kernels  252 us (93%)
  local copies, waits for them, and re-layouts  16.6 us (6%)
    pallas_call x1, Pallas kernels, forward_call(): pl.pallas_call(forward_kernel, name='forward_attention', out_shape=(sds((...  98.2 us
    pallas_call x1, Pallas kernels, backward_call(): pl.pallas_call(backward_kernel, name='backward_attention', out_shape=(sds...  95.3 us
    pallas_call x1, Pallas kernels, mlp_call(): pl.pallas_call(mlp_kernel, name='feed_forward', out_shape=(sds((rows, wid...  58.9 us
    unnamed x12, local copies, waits for them, and re-layouts  7.31 us
    concatenate x1, local copies, waits for them, and re-layouts, pack_vectors(): return jnp.concatenate(parts).reshape(8, 128).astype(F32)  5.42 us

profile of v1, /device:TPU:0, one launch (start us, length us, event | category | flops | bytes accessed | tf_op | source)
XLA Modules:
  0.0 270.4 jit_solution(8326607630921591236)
XLA Ops:
  0.7 5.4 %concatenate.3 = bf16[1024]{0:T(1024)(128)(2,1)S(1)} concatenate(bf16[32]{0:T(256)(128)(2,1)} %param.17, bf16[96]{0:T(256)(128)(2,1)S(1)} %broadcast.3, bf16[32]{0:T(256)(128)(2,1)} %param.18, bf16[96]{0:T(256)(128)(2,1)S(1)} %broadcast.3, bf16[32]{0:T(256)(128)(2,1)} %param.22, bf16[96]{0:T(256)(128)(2,1)S(1)} %broadcast.3, bf16[32]{0:T(256)(128)(2,1)} %param.23, ...), dimensions={0} | concatenate | bytes 4096 | tf_op jit(solution)/shard_map/concatenate | solution.py:374
  6.1 0.6 bitcast_convert_fusion.pack
  6.7 98.2 %forward_attention.1 = (bf16[128,1024]{1,0:T(8,128)(2,1)}, bf16[1024,128]{1,0:T(8,128)(2,1)}, bf16[2048,256]{1,0:T(8,128)(2,1)}, f32[2,1024]{1,0:T(2,128)}, bf16...) custom-call(bf16[128,1024]{1,0:T(8,128)(2,1)} %tok.5, ...), custom_call_target="tpu_custom_call" | custom-call | tf_op jit(solution)/shard_map/forward_attention/pallas_call | solution.py:335
  104.9 58.9 %feed_forward.1 = (bf16[128,1024]{1,0:T(8,128)(2,1)}, f32[128,1024]{1,0:T(8,128)}, bf16[128,1024]{1,0:T(8,128)(2,1)}, bf16[128,1024]{1,0:T(8,128)(2,1)}, bf16[51...) custom-call(bf16[128,1024]{1,0:T(8,128)(2,1)} %tok.5, ...), custom_call_target="tpu_custom_call" | custom-call | tf_op jit(solution)/shard_map/feed_forward/pallas_call | solution.py:509
  163.8 0.0 copy-start.2
  163.9 95.3 %backward_attention.1 = (bf16[128,1024]{1,0:T(8,128)(2,1)}, f32[128,1024]{1,0:T(8,128)}, f32[32,4096]{1,0:T(8,128)}, f32[32,3072]{1,0:T(8,128)}, f32[32,1024]{1,0:T(8,128)}, /*index=5*/f32[8,128]{1,0:T(8,128)}) custom-call(bf16[128,1024]{1,0:T(8,128)(2,1)} %tok.5, bf16[128,1024]{1,0:T(8,128)(2,1)} %get-tuple-element.44.gatt, ...), custom_call_target="tpu_custom_call" | custom-call | tf_op jit(solution)/shard_map/backward_attention/pallas_call | solution.py:800
  259.2 0.0 copy-start.1
  259.2 0.0 copy-start
  259.2 1.3 slice_bitcast_fusion.5
  260.5 1.2 slice_bitcast_fusion.1
  261.7 1.4 slice_bitcast_fusion
  263.1 0.0 copy-done.2
  263.1 0.7 copy.36
  263.8 1.7 copy.37
  265.5 1.8 copy.38
  267.2 1.6 copy.39
  268.8 0.0 copy-done.1
  268.8 0.8 copy.40
  269.6 0.0 copy-done
  269.6 0.8 copy.41
  (2 shorter events, 0.0 us)
Async XLA Ops:
  163.8 99.2 %copy-start.2 = (bf16[128,1024]{1,0:T(8,128)(2,1)S(1)}, bf16[128,1024]{1,0:T(8,128)(2,1)}, u32[]{:S(2)}) copy-start(bf16[128,1024]{1,0:T(8,128)(2,1)} %get-tuple-element.82) | copy-start | bytes 786436
  259.2 9.6 %copy-start.1 = (f32[32,4096]{1,0:T(8,128)S(1)}, f32[32,4096]{1,0:T(8,128)}, u32[]{:S(2)}) copy-start(f32[32,4096]{1,0:T(8,128)} %get-tuple-element.92) | copy-start | bytes 1572868
  259.2 10.4 %copy-start = (f32[128,1024]{1,0:T(8,128)S(1)}, f32[128,1024]{1,0:T(8,128)}, u32[]{:S(2)}) copy-start(f32[128,1024]{1,0:T(8,128)} %get-tuple-element.94) | copy-start | bytes 1572868

commit v2 on v0

--- a/solution.py
+++ b/solution.py
@@ -1,7 +1,816 @@
+import collections
+import functools
+
 import jax
 import jax.numpy as jnp
 from jax import lax
+from jax.experimental import pallas as pl
+from jax.experimental.pallas import tpu as pltpu
 from jax.sharding import PartitionSpec as P
+
+BF = jnp.bfloat16
+F32 = jnp.float32
+MESH = pl.DeviceIdType.MESH
+VMEM_LIMIT = 60 * 2**20
+NT = (((1,), (1,)), ((), ()))
+TN = (((0,), (0,)), ((), ()))
+NN = (((1,), (0,)), ((), ()))
+
+
+def dot(a, b, dims=NN):
+    return lax.dot_general(a, b, dims, preferred_element_type=F32)
+
+
+def flip(index, mask):
+    out = index
+    bit = 1
+    while bit <= mask:
+        if mask & bit:
+            out = out + bit - 2 * bit * ((index // bit) % 2)
+        bit *= 2
+    return out
+
+
+def ds(start, size, align=None):
+    if not isinstance(start, int):
+        start = pl.multiple_of(start, align or size)
+    return pl.ds(start, size)
+
+
+class Wire:
+    def __init__(self, ssem, rsem, lsem=None):
+        self.ssem, self.rsem, self.lsem = ssem, rsem, lsem
+        self.used = 0
+        self.local = 0
+        self.u = lax.axis_index("ulysses")
+        self.b = lax.axis_index("blk")
+        self.sent = []
+
+    def take(self, count):
+        first = self.used
+        self.used += count
+        return first
+
+    def make(self, src, dst, device, at, sent_at=None):
+        return pltpu.make_async_remote_copy(
+            src_ref=src,
+            dst_ref=dst,
+            send_sem=self.ssem.at[at if sent_at is None else sent_at],
+            recv_sem=self.rsem.at[at],
+            device_id=device,
+            device_id_type=MESH,
+        )
+
+    def blk(self, k, src, dst):
+        copy = self.make(src, dst, (self.u, flip(self.b, k)), self.take(1))
+        copy.start()
+        self.sent.append(copy)
+        return copy
+
+    def uly(self, k, src, dst):
+        copy = self.make(src, dst, (flip(self.u, k), self.b), self.take(1))
+        copy.start()
+        self.sent.append(copy)
+        return copy
+
+    def near(self, ku, kb, src, dst):
+        copy = self.make(src, dst, (flip(self.u, ku), flip(self.b, kb)), self.take(1))
+        copy.start()
+        self.sent.append(copy)
+        return copy
+
+    def here(self, src, dst):
+        copy = pltpu.make_async_copy(src, dst, self.lsem.at[self.local])
+        self.local += 1
+        copy.start()
+        return copy
+
+    def finish(self):
+        for copy in self.sent:
+            copy.wait_send()
+
+
+def greet(u, b, blk_masks, uly_masks, both=()):
+    barrier = pltpu.get_barrier_semaphore()
+    for k in blk_masks:
+        pl.semaphore_signal(barrier, inc=1, device_id=(u, flip(b, k)), device_id_type=MESH)
+    for k in uly_masks:
+        pl.semaphore_signal(barrier, inc=1, device_id=(flip(u, k), b), device_id_type=MESH)
+    for ku, kb in both:
+        pl.semaphore_signal(barrier, inc=1, device_id=(flip(u, ku), flip(b, kb)), device_id_type=MESH)
+    pl.semaphore_wait(barrier, len(blk_masks) + len(uly_masks) + len(both))
+
+
+def norm_parts(values):
+    center = jnp.mean(values, axis=-1, keepdims=True)
+    offset = values - center
+    spread = jnp.mean(offset * offset, axis=-1, keepdims=True)
+    inv = lax.rsqrt(spread + 1e-05)
+    return offset * inv, inv
+
+
+def head_mask(shape, head):
+    lane = lax.broadcasted_iota(jnp.int32, shape, len(shape) - 1)
+    return (lane // 64) == head
+
+
+def doc_begin(starts_ref, positions):
+    begin = jnp.zeros_like(positions)
+    for d in range(starts_ref.shape[0]):
+        first = starts_ref[d]
+        begin = jnp.where(positions >= first, jnp.full_like(positions, first), begin)
+    return begin
+
+
+def buffer_shapes(rows, width, hidden, heads):
+    group = 8 * rows
+    cols = 3 * heads
+    third = hidden // 4
+    return (
+        ("x_all", (group, width), BF),
+        ("n1", (group, width), BF),
+        ("q_out", (8, 32, cols), BF),
+        ("wqkv", (width, cols), BF),
+        ("up_out", (8, 32, hidden), BF),
+        ("wup", (4, 2, 128, hidden), BF),
+        ("wdown", (2, 2, rows, width), BF),
+        ("wproj", (4, 4, 2, 32, width), BF),
+        ("q", (group, heads), BF),
+        ("kv", (2 * group, 2 * heads), BF),
+        ("lse", (2, group), F32),
+        ("att_heads", (group, heads), BF),
+        ("att", (rows, width), BF),
+        ("par", (32, 8, 128), F32),
+        ("vec", (8, width), F32),
+        ("n2_all", (group, width), BF),
+        ("c_all", (group, width), BF),
+        ("act", (group, hidden), BF),
+        ("gup", (group, hidden), BF),
+        ("out_part", (group, width), BF),
+        ("g2_part", (group, width), BF),
+        ("out_sib", (4, rows, width), BF),
+        ("g2_sib", (4, rows, width), BF),
+        ("out_keep", (3, rows, width), BF),
+        ("g2_keep", (3, rows, width), BF),
+        ("out_far", (3, rows, width), BF),
+        ("g2_far", (3, rows, width), BF),
+        ("mixed", (rows, width), F32),
+        ("gmix", (rows, width), F32),
+        ("gbr", (rows, width), BF),
+        ("gatt", (rows, width), BF),
+        ("dwn", (2, 2, rows, width), BF),
+        ("dup", (4, 2, 128, hidden), BF),
+        ("dwn_y", (2, rows, width), BF),
+        ("dup_y", (2, 2, 128, hidden), BF),
+        ("dwn_keep", (2, rows, width), BF),
+        ("dup_keep", (2, 2, 128, hidden), BF),
+        ("dwn_z", (rows, width), BF),
+        ("dup_z", (2, 128, hidden), BF),
+        ("dup_own", (8, 32, hidden), BF),
+        ("gh", (group, heads), BF),
+        ("dkv", (2 * group, 2 * heads), F32),
+        ("halo_out", (group, 2 * heads), BF),
+        ("halo_in", (group, 2 * heads), BF),
+        ("gqkv", (group, cols), BF),
+        ("g1_part", (group, width), BF),
+        ("g1_sib", (4, rows, width), BF),
+        ("g1_keep", (3, rows, width), BF),
+        ("g1_far", (3, rows, width), BF),
+        ("dpr", (4, 4, 2, 32, width), BF),
+        ("dpr_sib", (4, 4, 32, width), BF),
+        ("dpr_keep", (4, 4, 32, width), BF),
+        ("dpr_u", (3, 4, 32, width), BF),
+        ("dpr_own", (4, 32, width), BF),
+        ("dpr_z", (3, 32, width), BF),
+        ("dq", (width, cols), BF),
+        ("dq_u", (3, 256, cols), BF),
+        ("dq_own", (8, 32, cols), BF),
+        ("sm", (32, 8, 128), F32),
+        ("sm_u", (3, 8, 8, 128), F32),
+        ("sm_keep", (8, 8, 128), F32),
+        ("sm_b", (7, 8, 128), F32),
+    )
+
+
+SEMAPHORES = 200
+
+
+def block_kernel(shapes, *refs):
+    (
+        tok, wqkv_in, wproj_in, wup_in, wdown_in, cot,
+        ln1_gain, ln1_bias, proj_bias, ln2_gain, ln2_bias, down_bias, qv_bias, up_bias_in, slopes, starts,
+    ) = refs[:16]
+    out_o, in_o, down_o, up_o, qkv_o, proj_o, vec_o = refs[16:23]
+    ssem, rsem, lsem = refs[23 + len(shapes):]
+    m = collections.namedtuple("Buffers", [s[0] for s in shapes])(*refs[23:23 + len(shapes)])
+
+    w = Wire(ssem, rsem, lsem)
+    u, b = w.u, w.b
+    z, c, zh = b // 2, b % 2, b // 4
+    x, y = u % 2, u // 2
+    rows, width = tok.shape
+    group = 8 * rows
+    pair = 2 * rows
+    rank = x * 4 + b % 4
+    chip2 = rank // 2
+    mine_b = ds(b * rows, rows)
+    mine_r = ds(rank * rows, rows)
+    at = u * 8 + b
+    m.par[at] = jnp.zeros((8, 128), F32)
+    for row, v in enumerate((ln1_gain, ln1_bias, proj_bias, ln2_gain, ln2_bias, down_bias, qv_bias, up_bias_in)):
+        m.par[at, row:row + 1, 0:v.shape[0]] = v[...].astype(F32).reshape(1, v.shape[0])
+    greet(u, b, range(1, 8), range(1, 4), [(1, k) for k in range(1, 4)])
+
+    p1 = [w.blk(k, m.par.at[at], m.par.at[at]) for k in range(1, 8)]
+    slot = m.x_all.at[mine_b]
+    t_z = {2: w.blk(4, tok, slot), 1: w.blk(2, tok, slot)}
+    t_sib = w.blk(1, tok, slot)
+    m.x_all[mine_b] = tok[...]
+    for r in range(8):
+        for part in range(3):
+            m.q_out[r, :, part * 128:(part + 1) * 128] = wqkv_in[
+                :, part * width + r * 128:part * width + (r + 1) * 128
+            ]
+    wrow = ds(at * 32, 32)
+    q1 = [w.blk(k, m.q_out.at[flip(b, k)], m.wqkv.at[wrow]) for k in range(1, 8)]
+    m.wqkv[wrow] = m.q_out[b]
+    for r in range(8):
+        for ch in range(4):
+            src = ((ch // 2) * 16 + (r // 4) * 8 + (ch % 2) * 4 + r % 4) * 128
+            m.up_out[r, :, ch * 128:(ch + 1) * 128] = wup_in[:, src:src + 128]
+    up_mine = m.wup.at[u, zh, ds((b % 4) * 32, 32)]
+    up1 = [w.near(k // 4, k % 4, m.up_out.at[flip(rank, k)], up_mine) for k in range(1, 8)]
+    l_up = w.here(m.up_out.at[rank], up_mine)
+    l_down = w.here(wdown_in, m.wdown.at[y, zh])
+    l_proj = w.here(wproj_in, m.wproj.at[u, z, c])
+
+    for copy in p1:
+        copy.wait_recv()
+    mine = m.par.at[ds(u * 8, 8)]
+    p2 = [w.uly(k, mine, mine) for k in range(1, 4)]
+    for copy in q1:
+        copy.wait_recv()
+    mine = m.wqkv.at[ds(u * 256, 256)]
+    q2 = [w.uly(k, mine, mine) for k in range(1, 4)]
+
+    fwd = {}
+
+    def to_sibling(k):
+        slot = m.x_all.at[ds(flip(b, 2 * k) * rows, rows)]
+        fwd[k] = w.blk(1, slot, slot)
+
+    t_z[2].wait_recv()
+    slot = m.x_all.at[ds(flip(b, 4) * rows, rows)]
+    t_z[3] = w.blk(2, slot, slot)
+    to_sibling(2)
+    d1 = w.blk(4, wdown_in, m.wdown.at[y, zh])
+    for copy in up1:
+        copy.wait_recv()
+    l_up.wait()
+    mine = m.wup.at[ds(y * 2, 2), zh]
+    up2 = w.blk(4, mine, mine)
+    pr1 = {k: w.blk(2 * k, wproj_in, m.wproj.at[u, z, c]) for k in (2, 1)}
+
+    for copy in p2:
+        copy.wait_recv()
+    for t in range(8):
+        tiles = [pltpu.roll(m.par[4 * t + k], 32 * k, 1) if k else m.par[4 * t] for k in range(4)]
+        m.vec[:, t * 128:(t + 1) * 128] = (tiles[0] + tiles[1]) + (tiles[2] + tiles[3])
+    vec = m.vec
+    q_bias = (m.par[2 * b] + pltpu.roll(m.par[2 * b + 1], 64, 1))[6:7]
+    v_bias = (m.par[16 + 2 * b] + pltpu.roll(m.par[17 + 2 * b], 64, 1))[6:7]
+    bias = jnp.concatenate([q_bias, jnp.zeros_like(q_bias), v_bias], axis=1)
+    up_bias = jnp.concatenate(
+        [m.par[(ch // 2) * 16 + x * 8 + (ch % 2) * 4 + b % 4][7:8] for ch in range(4)], axis=1
+    )
+
+    def normalize(zc):
+        at = ds(zc * pair, pair)
+        n, _ = norm_parts(m.x_all[at].astype(F32))
+        m.n1[at] = (n * vec[0:1] + vec[1:2]).astype(BF)
+
+    halo = w.take(4)
+    hand = []
+
+    def project(zc):
+        at = ds(zc * pair, pair)
+        out = (dot(m.n1[at], m.wqkv[...]) + bias).astype(BF)
+        m.q[at] = out[:, :128]
+        own = ds(group + zc * pair, pair)
+        m.kv[own] = out[:, 128:]
+        copy = w.make(m.kv.at[own], m.kv.at[at], (jnp.minimum(u + 1, 3), b), halo + zc)
+
+        @pl.when(u < 3)
+        def _():
+            copy.start()
+
+        hand.append(copy)
+
+    t_sib.wait_recv()
+    normalize(z)
+    t_z[1].wait_recv()
+    to_sibling(1)
+    fwd[2].wait_recv()
+    normalize(flip(z, 2))
+    for copy in q2:
+        copy.wait_recv()
+    project(z)
+    project(flip(z, 2))
+    fwd[1].wait_recv()
+    normalize(flip(z, 1))
+    project(flip(z, 1))
+    t_z[3].wait_recv()
+    to_sibling(3)
+    d1.wait_recv()
+    l_down.wait()
+    mine = m.wdown.at[y]
+    d2 = w.uly(2, mine, mine)
+    fwd[3].wait_recv()
+    normalize(flip(z, 3))
+    project(flip(z, 3))
+    pr1[2].wait_recv()
+    slot = m.wproj.at[u, flip(z, 2), c]
+    pr1[3] = w.blk(2, slot, slot)
+    up2.wait_recv()
+    mine = m.wup.at[ds(y * 2, 2)]
+    up3 = w.uly(2, mine, mine)
+
+    hops = ((0, 2), (1, 0), (1, 2))
+
+    def gather(src, buf):
+        slot = buf.at[mine_r]
+        return w.blk(1, src, slot), [w.near(ku, kb, src, slot) for ku, kb in hops]
+
+    def pass_on(copies, buf, i):
+        ku, kb = hops[i]
+        copies[i].wait_recv()
+        slot = buf.at[ds(flip(rank, ku * 4 + kb) * rows, rows)]
+        return w.blk(1, slot, slot)
+
+    c_sib, c_far = gather(cot, m.c_all)
+    m.c_all[mine_r] = cot[...]
+
+    @pl.when(u == 0)
+    def _():
+        m.kv[0:group] = jnp.zeros((group, 256), BF)
+
+    window = group + pair
+    krow = lax.broadcasted_iota(jnp.int32, (window, pair), 0)
+    qcol = lax.broadcasted_iota(jnp.int32, (window, pair), 1)
+    causal = krow - group <= qcol
+    kslope = (krow[:, :1] - group).astype(F32)
+    att_at = w.take(8)
+    lanes = ds(b * 128, 128)
+
+    def allowed_pairs(i):
+        qpos = lax.broadcasted_iota(jnp.int32, (1, pair), 1) + i * pair
+        begin = doc_begin(starts, qpos + u * group) - u * group - i * pair + group
+        return causal & (krow >= begin)
+
+    def attend(step, carry):
+        i = 3 - step
+
+        @pl.when(u > 0)
+        def _():
+            w.make(
+                m.kv.at[ds(i * pair, pair)], m.kv.at[ds(i * pair, pair)], (u, b), halo + i
+            ).wait_recv()
+
+        allowed = allowed_pairs(i)
+        span = ds(i * pair, window, pair)
+        keys = m.kv[span, 0:128]
+        vals = m.kv[span, 128:256]
+        at = ds(i * pair, pair)
+        query = m.q[at]
+        out = None
+        for h in range(2):
+            qh = jnp.where(head_mask((pair, 128), h), query, jnp.zeros_like(query))
+            s = dot(keys, qh, NT) * 0.125 + slopes[2 * b + h] * kslope
+            s = jnp.where(allowed, s, -1e30)
+            top = jnp.max(s, axis=0, keepdims=True)
+            p = jnp.exp(s - top)
+            total = jnp.sum(p, axis=0, keepdims=True)
+            m.lse[h:h + 1, at] = top + jnp.log(total)
+            o = dot(vals, p.astype(BF), TN) * (1.0 / total)
+            if h == 0:
+                out = o
+            else:
+                out = jnp.where(lax.broadcasted_iota(jnp.int32, o.shape, 0) < 64, out, o)
+        m.att_heads[at] = out.T.astype(BF)
+        for half in range(2):
+            target = 2 * i + half
+            piece = m.att_heads.at[ds(target * rows, rows)]
+
+            @pl.when(target != b)
+            def _():
+                w.make(piece, m.att.at[:, lanes], (u, target), att_at + b, att_at + target).start()
+
+        return carry
+
+    lax.fori_loop(0, 4, attend, 0)
+    m.att[:, lanes] = m.att_heads[mine_b]
+    pr1[1].wait_recv()
+    pr1[3].wait_recv()
+    l_proj.wait()
+    mine = m.wproj.at[u, :, c]
+    pr2 = [w.uly(k, mine, mine) for k in range(1, 4)]
+    c_fwd = [pass_on(c_far, m.c_all, i) for i in range(3)]
+    cot_f = cot[...].astype(F32)
+    down_bias_sum = jnp.sum(cot_f, axis=0, keepdims=True)
+    for copy in pr2:
+        copy.wait_recv()
+    mine = m.wproj.at[:, :, c]
+    pr3 = w.blk(1, mine, mine)
+    for k in range(1, 8):
+        other = flip(b, k)
+        w.make(
+            m.att_heads.at[ds(other * rows, rows)], m.att.at[:, ds(other * 128, 128)], (u, other), att_at + other
+        ).wait_recv()
+        w.make(
+            m.att_heads.at[ds(other * rows, rows)], m.att.at[:, lanes], (u, other), att_at + b, att_at + other
+        ).wait_send()
+    pr3.wait_recv()
+
+    wproj = m.wproj[...].reshape(width, width)
+    mixed = tok[...].astype(F32) + dot(m.att[...], wproj) + vec[2:3]
+    m.mixed[...] = mixed
+    n2, inv2 = norm_parts(mixed)
+    m.n2_all[mine_r] = (n2 * vec[3:4] + vec[4:5]).astype(BF)
+    n_sib, n_far = gather(m.n2_all.at[mine_r], m.n2_all)
+    up3.wait_recv()
+    d2.wait_recv()
+    hidden = m.act.shape[1]
+    wup = m.wup[...].reshape(width, hidden)
+    wdown = m.wdown[...].reshape(hidden, width)
+
+    def feed(chip):
+        at = ds(chip * pair, pair)
+        up = dot(m.n2_all[at], wup) + up_bias
+        square = up * up
+        th = jnp.tanh(0.7978845608028654 * (up + 0.044715 * square * up))
+        act = (0.5 * up * (1.0 + th)).astype(BF)
+        slope = 0.5 * (1.0 + th) + 0.5 * up * (1.0 - th * th) * (
+            0.7978845608028654 * (1.0 + 3.0 * 0.044715 * square)
+        )
+        gup = (dot(m.c_all[at], wdown, NT) * slope).astype(BF)
+        m.act[at] = act
+        m.gup[at] = gup
+        m.g2_part[at] = dot(gup, wup, NT).astype(BF)
+        m.out_part[at] = dot(act, wdown).astype(BF)
+
+    def swap(chip, i):
+        other = ds(chip * pair + (1 - c) * rows, rows)
+        return (
+            w.blk(1, m.g2_part.at[other], m.g2_sib.at[i]),
+            w.blk(1, m.out_part.at[other], m.out_sib.at[i]),
+        )
+
+    c_sib.wait_recv()
+    n_sib.wait_recv()
+    feed(chip2)
+    swaps = [swap(chip2, 3)]
+    g2_sends, out_sends = [], []
+
+    def merge(i):
+        ku, kb = hops[i]
+        far = flip(chip2, (ku * 4 + kb) // 2)
+        own = ds(far * pair + c * rows, rows)
+        swaps[i + 1][0].wait_recv()
+        m.g2_keep[i] = (m.g2_part[own].astype(F32) + m.g2_sib[i].astype(F32)).astype(BF)
+        g2_sends.append(w.near(ku, kb, m.g2_keep.at[i], m.g2_far.at[i]))
+
+    def merge_out(i):
+        ku, kb = hops[i]
+        far = flip(chip2, (ku * 4 + kb) // 2)
+        own = ds(far * pair + c * rows, rows)
+        swaps[i + 1][1].wait_recv()
+        m.out_keep[i] = (m.out_part[own].astype(F32) + m.out_sib[i].astype(F32)).astype(BF)
+        out_sends.append(w.near(ku, kb, m.out_keep.at[i], m.out_far.at[i]))
+
+    n_fwd = [pass_on(n_far, m.n2_all, 0)]
+    for i in range(3):
+        if i < 2:
+            n_fwd.append(pass_on(n_far, m.n2_all, i + 1))
+        c_fwd[i].wait_recv()
+        n_fwd[i].wait_recv()
+        ku, kb = hops[i]
+        far = flip(chip2, (ku * 4 + kb) // 2)
+        feed(far)
+        swaps.append(swap(far, i))
+        if i > 0:
+            merge(i - 1)
+    merge(2)
+    half = hidden // 2
+    for j in range(2):
+        span = slice(j * half, (j + 1) * half)
+        m.dwn[j] = dot(m.act[:, span], m.c_all[...], TN).astype(BF).reshape(2, rows, width)
+    y1 = w.uly(2, m.dwn.at[1 - y], m.dwn_y)
+    for j in range(2):
+        span = slice(j * half, (j + 1) * half)
+        m.dup[:, :, :, span] = dot(m.n2_all[...], m.gup[:, span], TN).astype(BF).reshape(4, 2, 128, half)
+    y2 = w.uly(2, m.dup.at[ds((1 - y) * 2, 2)], m.dup_y)
+    up_bias_sum = jnp.sum(m.gup[...].astype(F32), axis=0, keepdims=True)
+
+    own = ds(chip2 * pair + c * rows, rows)
+    swaps[0][0].wait_recv()
+    g = m.g2_part[own].astype(F32) + m.g2_sib[3].astype(F32)
+    for i in range(3):
+        g2_sends[i].wait_recv()
+        g = g + m.g2_far[i].astype(F32)
+    ln2_gain_sum = jnp.sum(g * n2, axis=0, keepdims=True)
+    ln2_bias_sum = jnp.sum(g, axis=0, keepdims=True)
+    e = g * vec[3:4]
+    gmix = cot_f + inv2 * (
+        e - jnp.mean(e, axis=-1, keepdims=True) - n2 * jnp.mean(e * n2, axis=-1, keepdims=True)
+    )
+    m.gmix[...] = gmix
+    proj_bias_sum = jnp.sum(gmix, axis=0, keepdims=True)
+    gbr = gmix.astype(BF)
+    m.gbr[...] = gbr
+    m.gatt[...] = dot(gbr, wproj, NT).astype(BF)
+
+    g_to = w.take(8)
+    g_sent = []
+    for k in range(1, 8):
+        other = flip(b, k)
+        copy = w.make(
+            m.gatt.at[:, ds(other * 128, 128)], m.gh.at[mine_b], (u, other), g_to + b, g_to + other
+        )
+        copy.start()
+        g_sent.append(copy)
+    m.gh[mine_b] = m.gatt[:, ds(b * 128, 128)]
+    for i in range(3):
+        merge_out(i)
+    for j in range(4):
+        m.dpr[j] = dot(m.att[:, j * 256:(j + 1) * 256], gbr, TN).astype(BF).reshape(4, 2, 32, width)
+    pg1 = w.blk(1, m.dpr.at[:, :, 1 - c], m.dpr_sib)
+    m.dkv[...] = jnp.zeros_like(m.dkv)
+    back = w.take(4)
+
+    def hand_back(i):
+        at = ds(i * pair, pair)
+        return w.make(m.halo_out.at[at], m.halo_in.at[at], (jnp.maximum(u - 1, 0), b), back + i)
+
+    def attend_back(i):
+        for half in range(2):
+            source = 2 * i + half
+
+            @pl.when(source != b)
+            def _():
+                w.make(
+                    m.gatt.at[:, lanes], m.gh.at[ds(source * rows, rows)], (u, b), g_to + source
+                ).wait_recv()
+
+        allowed = allowed_pairs(i)
+        span = slice(i * pair, i * pair + window)
+        at = slice(i * pair, (i + 1) * pair)
+        keys = m.kv[span, 0:128]
+        vals = m.kv[span, 128:256]
+        query = m.q[at]
+        grads = m.gh[at]
+        dk = dv = dq = None
+        for h in range(2):
+            mask = head_mask((pair, 128), h)
+            qh = jnp.where(mask, query, jnp.zeros_like(query))
+            gr = jnp.where(mask, grads, jnp.zeros_like(grads))
+            s = dot(keys, qh, NT) * 0.125 + slopes[2 * b + h] * kslope
+            p = jnp.where(allowed, jnp.exp(s - m.lse[h:h + 1, at]), 0.0)
+            dp = dot(vals, gr, NT)
+            delta = jnp.sum(p * dp, axis=0, keepdims=True)
+            gs = (p * (dp - delta)).astype(BF)
+            dv_h = dot(p.astype(BF), gr)
+            dk_h = dot(gs, qh)
+            dq_h = dot(keys, gs, TN)
+            if h == 0:
+                dk, dv, dq = dk_h, dv_h, dq_h
+            else:
+                dk, dv = dk + dk_h, dv + dv_h
+                dq = jnp.where(lax.broadcasted_iota(jnp.int32, dq.shape, 0) < 64, dq, dq_h)
+        m.gqkv[at, 0:128] = (dq.T * 0.125).astype(BF)
+        m.dkv[span, 0:128] += dk
+        m.dkv[span, 128:256] += dv
+        m.halo_out[at] = m.dkv[at].astype(BF)
+
+        @pl.when(u > 0)
+        def _():
+            hand_back(i).start()
+
+    attend_back(0)
+    attend_back(1)
+    pg1.wait_recv()
+    m.dpr_keep[...] = (m.dpr[:, :, c].astype(F32) + m.dpr_sib[...].astype(F32)).astype(BF)
+    pg2 = [w.uly(k, m.dpr_keep.at[flip(u, k)], m.dpr_u.at[k - 1]) for k in range(1, 4)]
+    y1.wait_recv()
+    m.dwn_keep[...] = (m.dwn[y].astype(F32) + m.dwn_y[...].astype(F32)).astype(BF)
+    z1 = w.blk(4, m.dwn_keep.at[1 - zh], m.dwn_z)
+    attend_back(2)
+    attend_back(3)
+    y2.wait_recv()
+    m.dup_keep[...] = (m.dup[ds(y * 2, 2)].astype(F32) + m.dup_y[...].astype(F32)).astype(BF)
+    z2 = w.blk(4, m.dup_keep.at[:, 1 - zh], m.dup_z)
+
+    for i in range(4):
+        at = slice(i * pair, (i + 1) * pair)
+        own = slice(group + i * pair, group + (i + 1) * pair)
+
+        @pl.when(u < 3)
+        def _():
+            w.make(m.halo_out.at[at], m.halo_in.at[at], (u, b), back + i).wait_recv()
+            m.dkv[own] += m.halo_in[at].astype(F32)
+
+        m.gqkv[at, 128:256] = (m.dkv[own, 0:128] * 0.125).astype(BF)
+        m.gqkv[at, 256:384] = m.dkv[own, 128:256].astype(BF)
+
+    swaps1 = {}
+
+    def spread(k):
+        chip = flip(z, k)
+        at = ds(chip * pair, pair)
+        m.g1_part[at] = dot(m.gqkv[at], m.wqkv[...], NT).astype(BF)
+        other = ds(chip * pair + (1 - c) * rows, rows)
+        swaps1[k] = w.blk(1, m.g1_part.at[other], m.g1_sib.at[k])
+
+    def chip_sum(k):
+        own = ds(flip(z, k) * pair + c * rows, rows)
+        swaps1[k].wait_recv()
+        return m.g1_part[own].astype(F32) + m.g1_sib[k].astype(F32)
+
+    spread(3)
+    spread(1)
+    m.g1_keep[2] = chip_sum(3).astype(BF)
+    via = w.blk(2, m.g1_keep.at[2], m.g1_far.at[2])
+    spread(2)
+    m.g1_keep[0] = chip_sum(1).astype(BF)
+    g1_near = w.blk(2, m.g1_keep.at[0], m.g1_far.at[0])
+    spread(0)
+    sum2 = chip_sum(2)
+    via.wait_recv()
+    m.g1_keep[1] = (sum2 + m.g1_far[2].astype(F32)).astype(BF)
+    g1_cross = w.blk(4, m.g1_keep.at[1], m.g1_far.at[1])
+    m.dq[...] = dot(m.n1[...], m.gqkv[...], TN).astype(BF)
+    q2g = [w.uly(k, m.dq.at[ds(flip(u, k) * 256, 256)], m.dq_u.at[k - 1]) for k in range(1, 4)]
+    qv_sums = jnp.sum(m.gqkv[...].astype(F32), axis=0, keepdims=True)
+
+    own = ds(chip2 * pair + c * rows, rows)
+    swaps[0][1].wait_recv()
+    out = m.mixed[...] + vec[5:6] + m.out_part[own].astype(F32) + m.out_sib[3].astype(F32)
+    for i in range(3):
+        out_sends[i].wait_recv()
+        out = out + m.out_far[i].astype(F32)
+    out_o[...] = out.astype(BF)
+    for copy in pg2:
+        copy.wait_recv()
+    m.dpr_own[...] = (
+        (m.dpr_keep[u].astype(F32) + m.dpr_u[0].astype(F32)) + (m.dpr_u[1].astype(F32) + m.dpr_u[2].astype(F32))
+    ).astype(BF)
+    pg3 = [w.blk(2 * k, m.dpr_own.at[flip(z, k)], m.dpr_z.at[k - 1]) for k in range(1, 4)]
+    z1.wait_recv()
+    down_o[...] = (m.dwn[y, zh].astype(F32) + m.dwn_y[zh].astype(F32)) + m.dwn_z[...].astype(F32)
+    z2.wait_recv()
+    m.dup_own[...] = (
+        (m.dup[ds(y * 2, 2), zh].astype(F32) + m.dup_y[:, zh].astype(F32)) + m.dup_z[...].astype(F32)
+    ).astype(BF).reshape(8, 32, hidden)
+    up3g = [w.near(k // 4, k % 4, m.dup_own.at[flip(rank, k)], up_o.at[rank]) for k in range(1, 8)]
+    up_o[rank] = m.dup_own[rank]
+    for copy in q2g:
+        copy.wait_recv()
+    m.dq_own[...] = (
+        (m.dq[ds(u * 256, 256)].astype(F32) + m.dq_u[0].astype(F32))
+        + (m.dq_u[1].astype(F32) + m.dq_u[2].astype(F32))
+    ).astype(BF).reshape(8, 32, 384)
+    q3g = [w.blk(k, m.dq_own.at[flip(b, k)], qkv_o.at[b]) for k in range(1, 8)]
+    qkv_o[b] = m.dq_own[b]
+
+    n, inv = norm_parts(tok[...].astype(F32))
+    g = chip_sum(0)
+    g1_near.wait_recv()
+    g1_cross.wait_recv()
+    g = g + m.g1_far[0].astype(F32) + m.g1_far[1].astype(F32)
+    lines = jnp.concatenate(
+        [
+            jnp.sum(g * n, axis=0, keepdims=True), jnp.sum(g, axis=0, keepdims=True),
+            proj_bias_sum, ln2_gain_sum, ln2_bias_sum, down_bias_sum, jnp.zeros((2, width), F32),
+        ],
+        axis=0,
+    )
+    for d in range(32):
+        m.sm[d] = lines[:, (d // 4) * 128:(d // 4 + 1) * 128]
+    for at, line in ((2 * b, qv_sums[:, 0:128]), (16 + 2 * b, qv_sums[:, 256:384])):
+        m.sm[at, 6:7] = line
+        m.sm[at + 1, 6:7] = line
+    for ch in range(4):
+        m.sm[(ch // 2) * 16 + x * 8 + (ch % 2) * 4 + b % 4, 7:8] = up_bias_sum[:, ch * 128:(ch + 1) * 128]
+    s1 = [w.uly(k, m.sm.at[ds(flip(u, k) * 8, 8)], m.sm_u.at[k - 1]) for k in range(1, 4)]
+    e = g * vec[0:1]
+    in_o[...] = (
+        m.gmix[...]
+        + inv * (e - jnp.mean(e, axis=-1, keepdims=True) - n * jnp.mean(e * n, axis=-1, keepdims=True))
+    ).astype(BF)
+    for copy in pg3:
+        copy.wait_recv()
+    proj_o[...] = (m.dpr_own[z].astype(F32) + m.dpr_z[0].astype(F32)) + (
+        m.dpr_z[1].astype(F32) + m.dpr_z[2].astype(F32)
+    )
+    for copy in s1:
+        copy.wait_recv()
+    m.sm_keep[...] = (m.sm[ds(u * 8, 8)] + m.sm_u[0]) + (m.sm_u[1] + m.sm_u[2])
+    s2 = [w.blk(k, m.sm_keep.at[flip(b, k)], m.sm_b.at[k - 1]) for k in range(1, 8)]
+    for copy in up3g + q3g + s2:
+        copy.wait_recv()
+    total = m.sm_keep[b]
+    for k in range(7):
+        total = total + m.sm_b[k]
+    line = lax.broadcasted_iota(jnp.int32, (8, 128), 0)
+    by32 = pltpu.roll(total, (128 - 32 * (b % 4)) % 128, 1)
+    by64 = pltpu.roll(total, (128 - 64 * (b % 2)) % 128, 1)
+    vec_o[...] = jnp.where(line < 6, by32, jnp.where(line == 6, by64, total))
+
+    for copy in g_sent:
+        copy.wait_send()
+
+    @pl.when(u < 3)
+    def _():
+        for copy in hand:
+            copy.wait_send()
+
+    @pl.when(u > 0)
+    def _():
+        for i in range(4):
+            hand_back(i).wait_send()
+
+    w.finish()
+
+
+def finish_kernel(
+    out, grad_in, down, up, qkv, proj, vec,
+    out_o, in_o, g1_o, b1_o, qkv_o, qv_o, proj_o, pb_o, g2_o, b2_o, up_o, ub_o, down_o, db_o,
+):
+    out_o[...] = out[...]
+    in_o[...] = grad_in[...]
+    down_o[...] = down[...]
+    proj_o[...] = proj[...]
+    for r in range(8):
+        for ch in range(4):
+            to = ((ch // 2) * 16 + (r // 4) * 8 + (ch % 2) * 4 + r % 4) * 128
+            up_o[:, to:to + 128] = up[r, :, ch * 128:(ch + 1) * 128].astype(F32)
+        for part in range(3):
+            to = part * 1024 + r * 128
+            qkv_o[:, to:to + 128] = qkv[r, :, part * 128:(part + 1) * 128].astype(F32)
+    for row, ref in enumerate((g1_o, b1_o, pb_o, g2_o, b2_o, db_o, qv_o, ub_o)):
+        ref[...] = vec[row, 0:ref.shape[0]]
+
+
+def fast_body(
+    tokens, ln1_gain, ln1_bias, qkv_weight, qv_bias, proj_weight, proj_bias, ln2_gain, ln2_bias,
+    up_weight, up_bias, down_weight, down_bias, alibi_slopes, doc_starts, cotangent,
+):
+    rows, width = tokens.shape
+    shapes = buffer_shapes(rows, width, 512, 128)
+    v = pl.BlockSpec(memory_space=pltpu.VMEM)
+    s = pl.BlockSpec(memory_space=pltpu.SMEM)
+    sds = jax.ShapeDtypeStruct
+    parts = pl.pallas_call(
+        functools.partial(block_kernel, shapes),
+        name="transformer_block",
+        out_shape=(
+            sds((rows, width), BF),
+            sds((rows, width), BF),
+            sds((rows, width), F32),
+            sds((8, 32, 512), BF),
+            sds((8, 32, 384), BF),
+            sds((32, width), F32),
+            sds((8, 128), F32),
+        ),
+        in_specs=[v] * 14 + [s, s],
+        out_specs=(v,) * 7,
+        scratch_shapes=[pltpu.VMEM(shape, kind) for _, shape, kind in shapes]
+        + [
+            pltpu.SemaphoreType.DMA((SEMAPHORES,)),
+            pltpu.SemaphoreType.DMA((SEMAPHORES,)),
+            pltpu.SemaphoreType.DMA((4,)),
+        ],
+        compiler_params=pltpu.CompilerParams(
+            collective_id=0, has_side_effects=True, vmem_limit_bytes=VMEM_LIMIT
+        ),
+    )(
+        tokens, qkv_weight, proj_weight, up_weight, down_weight, cotangent,
+        ln1_gain, ln1_bias, proj_bias, ln2_gain, ln2_bias, down_bias, qv_bias, up_bias,
+        alibi_slopes, doc_starts,
+    )
+    vector = sds((32,), F32)
+    return pl.pallas_call(
+        finish_kernel,
+        name="lay_out",
+        out_shape=(
+            sds((rows, width), BF), sds((rows, width), BF), vector, vector, sds((32, 3072), F32),
+            sds((64,), F32), sds((32, width), F32), vector, vector, vector, sds((32, 4096), F32),
+            sds((128,), F32), sds((rows, width), F32), vector,
+        ),
+        in_specs=[v] * 7,
+        out_specs=(v,) * 14,
+        compiler_params=pltpu.CompilerParams(vmem_limit_bytes=VMEM_LIMIT),
+    )(*parts)
+
 
 HEADS = 16
 HEAD_DIM = 64
@@ -47,7 +856,7 @@
     return (jnp.where(allowed[None], raw_scores, -1e30), allowed[None])
 
 
-def body(
+def general_body(
     tokens,
     ln1_gain,
     ln1_bias,
@@ -348,39 +1157,22 @@
     )
 
 
+TOKEN_ROWS = P(("ulysses", "blk"), None)
+VECTOR = P(("ulysses", "blk"))
+
+
 def solution(mesh):
+    whole = P()
     in_specs = (
-        P(("ulysses", "blk"), None),
-        P(("ulysses", "blk")),
-        P(("ulysses", "blk")),
-        P(("ulysses", "blk"), None),
-        P(("ulysses", "blk")),
-        P(("ulysses", "blk"), None),
-        P(("ulysses", "blk")),
-        P(("ulysses", "blk")),
-        P(("ulysses", "blk")),
-        P(("ulysses", "blk"), None),
-        P(("ulysses", "blk")),
-        P(("ulysses", "blk"), None),
-        P(("ulysses", "blk")),
-        P(),
-        P(),
-        P(("ulysses", "blk"), None),
+        TOKEN_ROWS, VECTOR, VECTOR, TOKEN_ROWS, VECTOR, TOKEN_ROWS, VECTOR, VECTOR, VECTOR, TOKEN_ROWS,
+        VECTOR, TOKEN_ROWS, VECTOR, whole, whole, TOKEN_ROWS,
     )
     out_specs = (
-        P(("ulysses", "blk"), None),
-        P(("ulysses", "blk"), None),
-        P(("ulysses", "blk")),
-        P(("ulysses", "blk")),
-        P(("ulysses", "blk"), None),
-        P(("ulysses", "blk")),
-        P(("ulysses", "blk"), None),
-        P(("ulysses", "blk")),
-        P(("ulysses", "blk")),
-        P(("ulysses", "blk")),
-        P(("ulysses", "blk"), None),
-        P(("ulysses", "blk")),
-        P(("ulysses", "blk"), None),
-        P(("ulysses", "blk")),
-    )
-    return jax.shard_map(body, mesh=mesh, in_specs=in_specs, out_specs=out_specs, check_vma=False)
+        TOKEN_ROWS, TOKEN_ROWS, VECTOR, VECTOR, TOKEN_ROWS, VECTOR, TOKEN_ROWS, VECTOR, VECTOR, VECTOR,
+        TOKEN_ROWS, VECTOR, TOKEN_ROWS, VECTOR,
+    )
+    fits = mesh.shape["ulysses"] == 4 and mesh.shape["blk"] == 8
+    return jax.shard_map(
+        fast_body if fits else general_body,
+        mesh=mesh, in_specs=in_specs, out_specs=out_specs, check_vma=False,
+    )

time: 1280 us -> 200 us (0.16); the launches traced: 1260 us -> 200 us
  waiting for transfers between devices: 558 us -> 0 us
  matrix products: 286 us -> 0 us
  Pallas kernels: 0 us -> 199 us
  blocking collectives: 195 us -> 0 us
  local copies, waits for them, and re-layouts: 119 us -> 0 us
  other arithmetic: 69.2 us -> 0 us
  loops' own time: 16.9 us -> 0 us
  between operations: 14.8 us -> 0.86 us
    reduce_scatter x4 -> x0, waiting for transfers between devices: 452 us -> none  [the longest x1 189 us: body(): lax.psum_scatter(up_grad, ('ulysses', 'blk'), scatter_dimension=0, tiled=...]
    dot_general x68 -> x0, matrix products: 286 us -> none  [the longest x24 76.9 us: score_block(): jnp.einsum('qhd,khd->hqk', queries, keys, preferred_element_type=jnp.floa...]
    pallas_call x0 -> x2, Pallas kernels: none -> 199 us  [the longest x1 196 us: fast_body(): pl.pallas_call(functools.partial(block_kernel, shapes), name='transformer...]
    all_gather x7 -> x0, waiting for transfers between devices: 103 us -> none  [the longest x1 42.9 us: body(): piece_rows = lax.all_gather(key_value, 'blk', axis=0, tiled=True)]
    unnamed x2 -> x0, blocking collectives: 82.6 us -> none
    all_gather x3 -> x0, blocking collectives: 70.3 us -> none  [the longest x1 40.9 us: body(): lax.all_gather(up_bias, ('ulysses', 'blk'), axis=0, tiled=True)]
    unnamed x100 -> x0, local copies, waits for them, and re-layouts: 42.2 us -> none
    all_to_all x3 -> x0, blocking collectives: 41.9 us -> none  [the longest x1 18 us: body(): lax.all_to_all(grad_pack.reshape(head_rows, 3, 1, features), 'ulysses', s...]
  transfers between devices with their start and end apart: 12 -> 0, of which waited for: 7 -> 0; matrix products, arithmetic and copies ran while one was open for 36% -> 0% of each run, Pallas kernels for 0% -> 0%
where the time goes in v2:
time: 200 us
  Pallas kernels  199 us (100%)
    pallas_call x1, Pallas kernels, fast_body(): pl.pallas_call(functools.partial(block_kernel, shapes), name='transformer...  196 us

profile of v2, /device:TPU:0, one launch (start us, length us, event | category | flops | bytes accessed | tf_op | source)
XLA Modules:
  0.0 199.5 jit_solution(562938789940235849)
XLA Ops:
  0.7 195.9 %transformer_block.1 = (bf16[128,1024]{1,0:T(8,128)(2,1)}, bf16[128,1024]{1,0:T(8,128)(2,1)}, f32[128,1024]{1,0:T(8,128)}, bf16[8,32,512]{2,1,0:T(8,128)(2,1)}, ...) custom-call(bf16[128,1024]{1,0:T(8,128)(2,1)} %refs_0_.1, bf16[32,3072]{1,0:T(8,128)(2,1)} %refs_1_.1, ...), custom_call_target="tpu_custom_call" | custom-call | tf_op jit(solution)/shard_map/transformer_block/pallas_call | solution.py:772
  196.5 2.8 %lay_out.1 = (bf16[128,1024]{1,0:T(8,128)(2,1)}, bf16[128,1024]{1,0:T(8,128)(2,1)}, f32[32]{0:T(128)}, f32[32]{0:T(128)}, f32[32,3072]{1,0:T(8,128)}, /*index=5*...) custom-call(bf16[128,1024]{1,0:T(8,128)(2,1)} %get-tuple-element.21., ...), custom_call_target="tpu_custom_call" | custom-call | tf_op jit(solution)/shard_map/lay_out/pallas_call | solution.py:801
